TPU v7x, 32 devices: a whole 2x2x4 slice. The times are simulated.
32 devices in a mesh: space: 8 (over z, x), bins: 4 (over y, core).
Axes of the slice: x: 2, y: 2, z: 4, core: 2. Of those that a mesh axis runs over, the one named last changes fastest.
Arguments:
- spectrum: bfloat16 [1152, 192, 64], P('bins', 'space'), may hold values from 0.099609375 to 2
- group_speed: float32 [2, 1152], P(None, 'bins'), may hold values from -0.3 to 0.3
- stokes_kernel: bfloat16 [1152, 128], P('bins'), may hold values from -0.1875 to 0.1875
- pair_bins: int32 [3, 4608], replicated, may hold values from 0 to 1151
- pair_coef: float32 [4608], replicated, may hold values from -3 to 3
- currents: float32 [64, 192, 128], P(('space', 'bins')), may hold values from -6 to 6
- col_map: int32 [32], replicated, may hold values from 0 to 31, each once
- wave_wet: int32 [192, 64], P('space'), may hold values 0 or 1
- ocean_wet: int32 [64, 192], P(('space', 'bins')), may hold values 0 or 1
Outputs:
- new_spectrum: bfloat16 [1152, 192, 64], P(None, ('space', 'bins'))
- new_currents: float32 [64, 192, 128], P(('space', 'bins'))
All inputs are finite; a program needn't handle non-finite values. No bound on the sum of `wave_wet` or of `ocean_wet` on one device may be relied on, other than what follows from the above.
Results may differ from a plain program's by a relative error of at most 0.0052.
Values may be sent and summed in bfloat16 or wider, within the bound.
A program may use at most 64 MiB of HBM per device.

v0:
```python
import jax
import jax.numpy as jnp
from jax import lax
from jax.sharding import PartitionSpec as P

DT_OCEAN = 0.5
CORIOLIS = 0.8
MIXING = 0.4
CURRENT_SCALE = 0.15
DT_SOURCE = 0.5


def for_sending(x):

    def short(part):
        return part.astype(jnp.bfloat16) if part.dtype == jnp.float32 else part

    return jax.tree.map(short, x)


def shifted(value, axis, steps):
    count = lax.axis_size(axis)
    first, last = (max(0, -steps), min(count, count - steps))
    return lax.ppermute(value, axis, [(source, source + steps) for source in range(first, last)])


def levels_laplacian(field):
    upper = jnp.concatenate([field[..., :1], field[..., :-1]], axis=-1)
    lower = jnp.concatenate([field[..., 1:], field[..., -1:]], axis=-1)
    return upper + lower - 2.0 * field


def ocean_step(currents, drift, wet, levels):
    east = currents[..., :levels]
    north = currents[..., levels:]
    east_drift = drift[..., :levels]
    north_drift = drift[..., levels:]
    new_east = east + DT_OCEAN * (
        CORIOLIS * (north + north_drift) + MIXING * levels_laplacian(east)
    )
    new_north = north + DT_OCEAN * (
        -CORIOLIS * (east + east_drift) + MIXING * levels_laplacian(north)
    )
    return wet[..., None].astype(jnp.float32) * jnp.concatenate([new_east, new_north], axis=-1)


def fluxes(energy, speeds, cur):
    speed_x = speeds[0][:, None, None] + cur[0][None]
    speed_y = speeds[1][:, None, None] + cur[1][None]
    plus_x = jnp.maximum(speed_x, 0.0) * energy
    minus_x = jnp.minimum(speed_x, 0.0) * energy
    plus_y = jnp.maximum(speed_y, 0.0) * energy
    minus_y = jnp.minimum(speed_y, 0.0) * energy
    return (plus_x, minus_x, plus_y, minus_y)


def combine(energy, flux_set, below, above, wet):
    plus_x, minus_x, plus_y, minus_y = flux_set
    plus_x_prev = jnp.concatenate([below[:, None, :], plus_x[:, :-1, :]], axis=1)
    minus_x_next = jnp.concatenate([minus_x[:, 1:, :], above[:, None, :]], axis=1)
    plus_y_prev = jnp.pad(plus_y[:, :, :-1], ((0, 0), (0, 0), (1, 0)))
    minus_y_next = jnp.pad(minus_y[:, :, 1:], ((0, 0), (0, 0), (0, 1)))
    moved = energy.astype(jnp.float32) - plus_x + plus_x_prev - minus_x_next + minus_x
    moved = moved - plus_y + plus_y_prev - minus_y_next + minus_y
    return (wet.astype(jnp.float32)[None] * moved).astype(jnp.bfloat16)


def per_device(
    spectrum,
    group_speed,
    stokes_kernel,
    pair_bins,
    pair_coef,
    currents,
    col_map,
    wave_wet,
    ocean_wet,
):
    local_bins, tile_rows, columns = spectrum.shape
    space_count = lax.axis_size("space")
    bins_count = lax.axis_size("bins")
    groups = space_count * bins_count
    group_cols = columns // groups
    levels = stokes_kernel.shape[1] // 2
    block_rows = tile_rows // bins_count
    slot_col = (
        col_map[:, None] * group_cols + jnp.arange(group_cols, dtype=jnp.int32)[None, :]
    ).reshape(-1)
    inverse = jnp.argsort(slot_col)
    pair_total = pair_bins.shape[1]
    block_pairs = pair_total // 4
    first_bins = pair_bins[0].reshape(4, block_pairs)
    second_bins = pair_bins[1].reshape(4, block_pairs)
    target_bins = pair_bins[2].reshape(4, block_pairs)
    coef_blocks = pair_coef.reshape(4, block_pairs)
    cells = lax.all_to_all(spectrum, "bins", split_axis=1, concat_axis=0, tiled=True)
    kernel_all, speeds_all = (
        lax.all_gather(
            stokes_kernel.astype(jnp.float32).astype(jnp.bfloat16), "bins", axis=0, tiled=True
        ).astype(jnp.float32),
        lax.all_gather(group_speed.astype(jnp.bfloat16), "bins", axis=1, tiled=True).astype(
            group_speed.dtype
        ),
    )
    kernel_all = kernel_all.astype(jnp.bfloat16)
    partial_value = jnp.einsum("kxc,kl->cxl", cells, kernel_all, preferred_element_type=jnp.float32)
    routed = jnp.take(partial_value, slot_col, axis=0)
    drift = lax.all_to_all(
        routed.astype(jnp.bfloat16), ("space", "bins"), split_axis=0, concat_axis=1, tiled=True
    ).astype(routed.dtype)
    new_currents = ocean_step(currents, drift, ocean_wet, levels)
    surface = jnp.stack([new_currents[:, :, 0], new_currents[:, :, levels]])
    slotted = lax.all_to_all(surface, ("space", "bins"), split_axis=2, concat_axis=1, tiled=True)
    cur = CURRENT_SCALE * jnp.tanh(jnp.transpose(jnp.take(slotted, inverse, axis=1), (0, 2, 1)))
    wet_rows = lax.dynamic_slice_in_dim(
        wave_wet, lax.axis_index("bins") * block_rows, block_rows, 0
    )
    flux_set = fluxes(cells, speeds_all, cur)
    below = shifted(for_sending(flux_set[0][:, -1, :]), ("space", "bins"), 1)
    above = shifted(for_sending(flux_set[1][:, 0, :]), ("space", "bins"), -1)
    advected = combine(cells, flux_set, below, above, wet_rows)
    all_bins, some_rows, some_cols = advected.shape
    flat = advected.reshape(all_bins, some_rows * some_cols)
    bin_ids = jnp.arange(all_bins, dtype=jnp.int32)

    def one_block(total, tables):
        first_ids, second_ids, target_ids, coefs = tables
        first = jnp.take(flat, first_ids, axis=0).astype(jnp.float32)
        second = jnp.take(flat, second_ids, axis=0).astype(jnp.float32)
        products = (coefs[:, None] * first * second).astype(jnp.bfloat16)
        onehot = (bin_ids[:, None] == target_ids[None, :]).astype(jnp.bfloat16)
        return (total + jnp.dot(onehot, products, preferred_element_type=jnp.float32), None)

    start = jnp.zeros((all_bins, some_rows * some_cols), jnp.float32)
    source, _ = lax.scan(one_block, start, (first_bins, second_bins, target_bins, coef_blocks))
    updated = (flat.astype(jnp.float32) + DT_SOURCE * source).astype(jnp.bfloat16)
    new_spectrum = updated.reshape(all_bins, some_rows, some_cols)
    return (new_spectrum, new_currents)


def solution(mesh):
    placed = (
        P("bins", "space", None),
        P(None, "bins"),
        P("bins", None),
        P(),
        P(),
        P(("space", "bins"), None, None),
        P(),
        P("space", None),
        P(("space", "bins"), None),
    )
    return jax.shard_map(
        per_device,
        mesh=mesh,
        in_specs=placed,
        out_specs=(P(None, ("space", "bins"), None), P(("space", "bins"), None, None)),
        check_vma=False,
    )
```

profile of v0, /device:TPU:1, one launch (start us, length us, event | category | flops | bytes accessed | tf_op | source)
XLA Modules:
  0.0 127.7 jit_solution(9447055608251418342)
XLA Ops:
  0.6 4.4 %all-to-all-start = ((bf16[288,24,64]{0,2,1:T(8,128)(2,1)}), bf16[288,24,64]{0,2,1:T(8,128)(2,1)S(1)}, u32[]{:S(2)}, u32[]{:S(2)}) async-start(bf16[288,24,64]{0,2,1:T(8,128)(2,1)} %param.13), calls=%async_computation | async-start | bytes 2359296 | tf_op jit(solution)/shard_map/all_to_all | solution.py:96
  5.3 0.6 add.154
  6.5 0.6 pad_clamp_fusion.3
  7.4 0.8 copy.133
  8.2 0.8 copy.134
  9.2 0.7 copy.132
  9.9 0.7 copy.135
  10.6 0.8 copy.124
  11.5 0.6 convert_element_type.86
  12.1 2.0 %sort.17 = (s32[64]{0:T(128)}, s32[64]{0:T(128)S(1)}) sort(s32[64]{0:T(128)S(1)} %copy-done.12, s32[64]{0:T(128)S(1)} %iota.11), dimensions={0}, to_apply=%region_0.0 | sort | flops 384 | bytes 1024 | tf_op jit(solution)/shard_map/jit(argsort)/sort | solution.py:89
  14.1 0.5 copy-done.14
  14.7 7.0 %all-gather = bf16[4,288,2]{1,2,0:T(2,128)(2,1)S(1)} all-gather(bf16[1,288,2]{1,2,0:T(2,128)(2,1)S(1)} %convert_bitcast_fusion), channel_id=1, replica_groups=mesh['space'=8,'bins'=4] {'bins'}, dimensions={0}, use_global_device_ids=true | all-gather | bytes 5760 | tf_op jit(solution)/shard_map/all_gather | solution.py:101
  21.8 6.0 %all_gather.7 = bf16[1152,128]{1,0:T(8,128)(2,1)S(1)} all-gather(bf16[288,128]{1,0:T(8,128)(2,1)S(1)} %copy-done.4), channel_id=1, replica_groups=mesh['space'=8,'bins'=4] {'bins'}, dimensions={0}, use_global_device_ids=true | all-gather | bytes 368640 | tf_op jit(solution)/shard_map/all_gather | solution.py:98
  28.1 0.9 copy.140
  29.0 0.7 reshape.131
  30.3 0.9 gather_fusion.2
  31.2 0.8 select_convert_fusion
  32.0 5.5 %all-to-all-start.1 = ((bf16[64,6,128]{2,1,0:T(8,128)(2,1)}), bf16[64,6,128]{2,1,0:T(8,128)(2,1)S(1)}, u32[]{:S(2)}, u32[]{:S(2)}) async-start(bf16[64,6,128]{2,1,0:T(8,128)(2,1)} %select_convert_fusion), calls=%async_computation.1 | async-start | bytes 262144 | tf_op jit(solution)/shard_map/all_to_all | solution.py:108
  37.6 8.2 %all-to-all-done.1 = bf16[64,6,128]{2,1,0:T(8,128)(2,1)S(1)} async-done(((bf16[64,6,128]{2,1,0:T(8,128)(2,1)}), bf16[64,6,128]{2,1,0:T(8,128)(2,1)S(1)}, u32[]{:S(2)}, u32[]{:S(2)}) %all-to-all-start.1) | async-done | bytes 98336 | tf_op jit(solution)/shard_map/all_to_all | solution.py:108
  46.6 0.8 copy.111
  47.4 2.5 %all-to-all-start.2 = ((f32[2,2,192]{1,0,2:T(2,128)}), f32[2,2,192]{1,0,2:T(2,128)S(1)}, u32[]{:S(2)}, u32[]{:S(2)}) async-start(f32[2,2,192]{1,0,2:T(2,128)} %copy.111), calls=%async_computation.2 | async-start | bytes 393216 | tf_op jit(solution)/shard_map/all_to_all | solution.py:113
  49.9 0.7 dynamic-slice_convert_fusion
  50.7 0.7 all_to_all.36
  51.5 0.8 copy.120
  52.3 7.0 %all-to-all-done.2 = f32[2,2,192]{1,0,2:T(2,128)S(1)} async-done(((f32[2,2,192]{1,0,2:T(2,128)}), f32[2,2,192]{1,0,2:T(2,128)S(1)}, u32[]{:S(2)}, u32[]{:S(2)}) %all-to-all-start.2) | async-done | bytes 3104 | tf_op jit(solution)/shard_map/all_to_all | solution.py:113
  59.3 0.5 copy.121
  59.9 0.7 gather_fusion.3
  60.9 0.7 convert_multiply_fusion.1
  61.7 1.9 %collective-permute-start.1 = (bf16[1152,64]{0,1:T(8,128)(2,1)S(1)}, bf16[1152,64]{0,1:T(8,128)(2,1)S(1)}, u32[]{:S(2)}, u32[]{:S(2)}) collective-permute-start(bf16[1152,64]{0,1:T(8,128)(2,1)S(1)} %fusion.22), channel_id=1, source_target_pairs={{1,0},{2,1},{3,2},{4,3},{5,4},{6,5},{7,6},{8,7},{9,8},{10,9},{11,1... | collective-permute-start | bytes 442376 | tf_op jit(solution)/shard_map/ppermute | solution.py:24
  64.0 3.8 %collective-permute-start = (bf16[1152,64]{0,1:T(8,128)(2,1)S(1)}, bf16[1152,64]{0,1:T(8,128)(2,1)S(1)}, u32[]{:S(2)}, u32[]{:S(2)}) collective-permute-start(bf16[1152,64]{0,1:T(8,128)(2,1)S(1)} %fusion.21), channel_id=1, source_target_pairs={{0,1},{1,2},{2,3},{3,4},{4,5},{5,6},{6,7},{7,8},{8,9},{9,10},{10,1... | collective-permute-start | bytes 442376 | tf_op jit(solution)/shard_map/ppermute | solution.py:24
  68.2 1.5 %collective-permute-done = bf16[1152,64]{0,1:T(8,128)(2,1)S(1)} collective-permute-done((bf16[1152,64]{0,1:T(8,128)(2,1)S(1)}, bf16[1152,64]{0,1:T(8,128)(2,1)S(1)}, u32[]{:S(2)}, u32[]{:S(2)}) %collective-permute-start) | collective-permute-done | bytes 147488 | tf_op jit(solution)/shard_map/ppermute | solution.py:24
  69.7 2.0 %fusion.20 = bf16[1152,6,64]{0,2,1:T(8,128)(2,1)S(1)} fusion(bf16[1152,6,64]{0,2,1:T(8,128)(2,1)S(1)} %all_to_all.36, f32[1152,5,64]{0,2,1:T(8,128)S(1)} %slice.133, f32[1152,1,64]{0,2,1:T(8,128)S(1)} %bitcast_convert_fusion.1, f32[1152,1,64]{0,2,1:T(8,128)S(1)} %bitcast_convert_fusion, f32[1152,5,64]{0,2,1:T(8,128)S(1)} %slice.134, ...), kind=kLoop, calls=%fused_computation.44 | loop fusion | flops 10174464 | bytes 8805888 | tf_op jit(solution)/shard_map/convert_element_type | solution.py:65
  71.8 0.9 copy.117
  72.6 51.9 %while.11 = (s32[]{:T(128)}, f32[1152,384]{1,0:T(8,128)}, s32[4,1152]{1,0:T(4,128)S(1)}, f32[4,1152]{1,0:T(4,128)S(1)}, s32[4,1152]{1,0:T(4,128)S(1)}, /*index=5...) while((s32[]{:T(128)}, f32[1152,384]{1,0:T(8,128)}, ...), condition=%wide.region_2.4_spmd.clone, body=%wide.region_1.3_spmd.clone.sunk | while | flops 1024549120 | bytes 8960627 | solution.py:135
  72.7 4.3 %gather_fusion = bf16[1152,384]{1,0:T(8,128)(2,1)S(1)} fusion(bf16[1152,384]{1,0:T(8,128)(2,1)S(1)} %get-tuple-element.234, s32[2048]{0:T(1024)S(1)} %pad_clamp_fusion.6), kind=kCustom, calls=%fused_computation.1.clone.clone.1 | custom fusion | bytes 1774080 | tf_op jit(solution)/shard_map/while/body/eval_jaxpr/jit(_take)/gather | solution.py:129
  77.0 4.3 %gather_fusion.1 = bf16[1152,384]{1,0:T(8,128)(2,1)S(1)} fusion(bf16[1152,384]{1,0:T(8,128)(2,1)S(1)} %get-tuple-element.234, s32[2048]{0:T(1024)S(1)} %pad_clamp_fusion.7), kind=kCustom, calls=%fused_computation.clone.clone.1 | custom fusion | bytes 1774080 | tf_op jit(solution)/shard_map/while/body/eval_jaxpr/jit(_take)/gather | solution.py:128
  81.4 3.1 %fusion.44 = f32[1152,384]{1,0:T(8,128)} fusion(s32[1152]{0:T(1024)S(1)} %dynamic-slice_reduce_fusion.7, f32[1152,384]{1,0:T(8,128)} %get-tuple-element.221, bf16[1152,384]{1,0:T(8,128)(2,1)S(1)} %gather_fusion, bf16[1152,384]{1,0:T(8,128)(2,1)S(1)} %gather_fusion.1, f32[1152]{0:T(1024)S(1)} %dynamic-slice_reduce_fusion.9, ...), kind=kOutput, calls=%fused_computation.7.clone.1 | convolution fusion | flops 1024524288 | bytes 5319937 | tf_op jit(solution)/shard_map/while/body/eval_jaxpr/dot_general | solution.py:132
  84.6 4.3 %gather_fusion = bf16[1152,384]{1,0:T(8,128)(2,1)S(1)} fusion(bf16[1152,384]{1,0:T(8,128)(2,1)S(1)} %get-tuple-element.234, s32[2048]{0:T(1024)S(1)} %pad_clamp_fusion.6), kind=kCustom, calls=%fused_computation.1.clone.clone.1 | custom fusion | bytes 1774080 | tf_op jit(solution)/shard_map/while/body/eval_jaxpr/jit(_take)/gather | solution.py:129
  88.9 4.3 %gather_fusion.1 = bf16[1152,384]{1,0:T(8,128)(2,1)S(1)} fusion(bf16[1152,384]{1,0:T(8,128)(2,1)S(1)} %get-tuple-element.234, s32[2048]{0:T(1024)S(1)} %pad_clamp_fusion.7), kind=kCustom, calls=%fused_computation.clone.clone.1 | custom fusion | bytes 1774080 | tf_op jit(solution)/shard_map/while/body/eval_jaxpr/jit(_take)/gather | solution.py:128
  93.3 4.6 %fusion.44 = f32[1152,384]{1,0:T(8,128)} fusion(s32[1152]{0:T(1024)S(1)} %dynamic-slice_reduce_fusion.7, f32[1152,384]{1,0:T(8,128)} %get-tuple-element.221, bf16[1152,384]{1,0:T(8,128)(2,1)S(1)} %gather_fusion, bf16[1152,384]{1,0:T(8,128)(2,1)S(1)} %gather_fusion.1, f32[1152]{0:T(1024)S(1)} %dynamic-slice_reduce_fusion.9, ...), kind=kOutput, calls=%fused_computation.7.clone.1 | convolution fusion | flops 1024524288 | bytes 5319937 | tf_op jit(solution)/shard_map/while/body/eval_jaxpr/dot_general | solution.py:132
  97.9 4.3 %gather_fusion = bf16[1152,384]{1,0:T(8,128)(2,1)S(1)} fusion(bf16[1152,384]{1,0:T(8,128)(2,1)S(1)} %get-tuple-element.234, s32[2048]{0:T(1024)S(1)} %pad_clamp_fusion.6), kind=kCustom, calls=%fused_computation.1.clone.clone.1 | custom fusion | bytes 1774080 | tf_op jit(solution)/shard_map/while/body/eval_jaxpr/jit(_take)/gather | solution.py:129
  102.2 4.3 %gather_fusion.1 = bf16[1152,384]{1,0:T(8,128)(2,1)S(1)} fusion(bf16[1152,384]{1,0:T(8,128)(2,1)S(1)} %get-tuple-element.234, s32[2048]{0:T(1024)S(1)} %pad_clamp_fusion.7), kind=kCustom, calls=%fused_computation.clone.clone.1 | custom fusion | bytes 1774080 | tf_op jit(solution)/shard_map/while/body/eval_jaxpr/jit(_take)/gather | solution.py:128
  106.6 4.6 %fusion.44 = f32[1152,384]{1,0:T(8,128)} fusion(s32[1152]{0:T(1024)S(1)} %dynamic-slice_reduce_fusion.7, f32[1152,384]{1,0:T(8,128)} %get-tuple-element.221, bf16[1152,384]{1,0:T(8,128)(2,1)S(1)} %gather_fusion, bf16[1152,384]{1,0:T(8,128)(2,1)S(1)} %gather_fusion.1, f32[1152]{0:T(1024)S(1)} %dynamic-slice_reduce_fusion.9, ...), kind=kOutput, calls=%fused_computation.7.clone.1 | convolution fusion | flops 1024524288 | bytes 5319937 | tf_op jit(solution)/shard_map/while/body/eval_jaxpr/dot_general | solution.py:132
  111.3 4.3 %gather_fusion = bf16[1152,384]{1,0:T(8,128)(2,1)S(1)} fusion(bf16[1152,384]{1,0:T(8,128)(2,1)S(1)} %get-tuple-element.234, s32[2048]{0:T(1024)S(1)} %pad_clamp_fusion.6), kind=kCustom, calls=%fused_computation.1.clone.clone.1 | custom fusion | bytes 1774080 | tf_op jit(solution)/shard_map/while/body/eval_jaxpr/jit(_take)/gather | solution.py:129
  115.6 4.3 %gather_fusion.1 = bf16[1152,384]{1,0:T(8,128)(2,1)S(1)} fusion(bf16[1152,384]{1,0:T(8,128)(2,1)S(1)} %get-tuple-element.234, s32[2048]{0:T(1024)S(1)} %pad_clamp_fusion.7), kind=kCustom, calls=%fused_computation.clone.clone.1 | custom fusion | bytes 1774080 | tf_op jit(solution)/shard_map/while/body/eval_jaxpr/jit(_take)/gather | solution.py:128
  120.0 4.6 %fusion.44 = f32[1152,384]{1,0:T(8,128)} fusion(s32[1152]{0:T(1024)S(1)} %dynamic-slice_reduce_fusion.7, f32[1152,384]{1,0:T(8,128)} %get-tuple-element.221, bf16[1152,384]{1,0:T(8,128)(2,1)S(1)} %gather_fusion, bf16[1152,384]{1,0:T(8,128)(2,1)S(1)} %gather_fusion.1, f32[1152]{0:T(1024)S(1)} %dynamic-slice_reduce_fusion.9, ...), kind=kOutput, calls=%fused_computation.7.clone.1 | convolution fusion | flops 1024524288 | bytes 5319937 | tf_op jit(solution)/shard_map/while/body/eval_jaxpr/dot_general | solution.py:132
  124.5 1.7 %add_convert_fusion = bf16[1152,384]{1,0:T(8,128)(2,1)S(1)} fusion(f32[1152,384]{1,0:T(8,128)} %get-tuple-element.47, bf16[1152,384]{1,0:T(8,128)(2,1)S(1)} %get-tuple-element.238), kind=kLoop, calls=%fused_computation.45 | loop fusion | flops 1769472 | bytes 3538944 | tf_op jit(solution)/shard_map/convert_element_type | solution.py:136
  126.2 1.5 %copy.119 = bf16[1152,384]{0,1:T(8,128)(2,1)} copy(bf16[1152,384]{1,0:T(8,128)(2,1)S(1)} %add_convert_fusion) | data formatting | bytes 1769472 | tf_op jit(solution)/shard_map/convert_element_type | solution.py:136
  (120 shorter events, 4.7 us)
Async XLA Ops:
  0.6 4.5 %copy-start.13 = (s32[32]{0:T(128)S(1)}, s32[32]{0:T(128)}, u32[]{:S(2)}) copy-start(s32[32]{0:T(128)} %param.19) | copy-start | bytes 388
  0.6 5.3 %copy-start = (f32[2,192,128]{2,1,0:T(8,128)S(1)}, f32[2,192,128]{2,1,0:T(8,128)}, u32[]{:S(2)}) copy-start(f32[2,192,128]{2,1,0:T(8,128)} %param.18) | copy-start | bytes 589828
  0.6 27.4 %all-to-all-start = ((bf16[288,24,64]{0,2,1:T(8,128)(2,1)}), bf16[288,24,64]{0,2,1:T(8,128)(2,1)S(1)}, u32[]{:S(2)}, u32[]{:S(2)}) async-start(bf16[288,24,64]{0,2,1:T(8,128)(2,1)} %param.13), calls=%async_computation | async-start | bytes 2359296 | tf_op jit(solution)/shard_map/all_to_all | solution.py:96
  6.3 15.4 %copy-start.4 = (bf16[288,128]{1,0:T(8,128)(2,1)S(1)}, bf16[288,128]{1,0:T(8,128)(2,1)}, u32[]{:S(2)}) copy-start(bf16[288,128]{1,0:T(8,128)(2,1)} %param.15) | copy-start | bytes 221188
  6.5 5.0 %copy-start.11 = (s32[2,192]{1,0:T(2,128)S(1)}, s32[2,192]{1,0:T(2,128)}, u32[]{:S(2)}) copy-start(s32[2,192]{1,0:T(2,128)} %param.21) | copy-start | bytes 4612
  6.5 5.6 %copy-start.12 = (s32[64]{0:T(128)S(1)}, s32[64]{0:T(128)}, u32[]{:S(2)}) copy-start(s32[64]{0:T(128)} %add.154) | copy-start | bytes 772
  6.5 8.2 %copy-start.10 = (f32[2,288]{1,0:T(2,128)S(1)}, f32[2,288]{1,0:T(2,128)}, u32[]{:S(2)}) copy-start(f32[2,288]{1,0:T(2,128)} %param.14) | copy-start | bytes 6916
  6.5 21.4 %copy-start.5 = (s32[3,4608]{1,0:T(4,128)S(1)}, s32[3,4608]{1,0:T(4,128)}, u32[]{:S(2)}) copy-start(s32[3,4608]{1,0:T(4,128)} %param.16) | copy-start | bytes 165892
  14.1 0.5 copy-start.14
  29.0 8.6 %copy-start.15 = (s32[64]{0:T(128)S(1)}, s32[64]{0:T(128)}, u32[]{:S(2)}) copy-start(s32[64]{0:T(128)} %copy-done.14) | copy-start | bytes 772
  30.1 16.2 %copy-start.1 = (f32[2,192,63]{1,2,0:T(8,128)S(1)}, f32[2,192,63]{1,2,0:T(8,128)}, u32[]{:S(2)}) copy-start(f32[2,192,63]{1,2,0:T(8,128)} %copy.133) | copy-start | bytes 290308
  30.2 16.2 %copy-start.2 = (f32[2,192,63]{1,2,0:T(8,128)S(1)}, f32[2,192,63]{1,2,0:T(8,128)}, u32[]{:S(2)}) copy-start(f32[2,192,63]{1,2,0:T(8,128)} %copy.134) | copy-start | bytes 290308
  30.2 16.2 %copy-start.3 = (f32[2,192,64]{1,2,0:T(8,128)S(1)}, f32[2,192,64]{1,2,0:T(8,128)}, u32[]{:S(2)}) copy-start(f32[2,192,64]{1,2,0:T(8,128)} %copy.124) | copy-start | bytes 294916
  30.2 16.2 %copy-start.7 = (f32[2,192,1]{1,2,0:T(1,128)S(1)}, f32[2,192,1]{1,2,0:T(1,128)}, u32[]{:S(2)}) copy-start(f32[2,192,1]{1,2,0:T(1,128)} %copy.132) | copy-start | bytes 4612
  30.2 16.2 %copy-start.8 = (f32[2,192,1]{1,2,0:T(1,128)S(1)}, f32[2,192,1]{1,2,0:T(1,128)}, u32[]{:S(2)}) copy-start(f32[2,192,1]{1,2,0:T(1,128)} %copy.135) | copy-start | bytes 4612
  31.2 15.3 %copy-start.9 = (f32[2,192]{1,0:T(2,128)S(1)}, f32[2,192]{1,0:T(2,128)}, u32[]{:S(2)}) copy-start(f32[2,192]{1,0:T(2,128)} %convert_element_type.86) | copy-start | bytes 4612
  32.0 13.7 %all-to-all-start.1 = ((bf16[64,6,128]{2,1,0:T(8,128)(2,1)}), bf16[64,6,128]{2,1,0:T(8,128)(2,1)S(1)}, u32[]{:S(2)}, u32[]{:S(2)}) async-start(bf16[64,6,128]{2,1,0:T(8,128)(2,1)} %select_convert_fusion), calls=%async_computation.1 | async-start | bytes 262144 | tf_op jit(solution)/shard_map/all_to_all | solution.py:108
  46.1 4.6 %copy-start.6 = (f32[4608]{0:T(1024)S(1)}, f32[4608]{0:T(1024)}, u32[]{:S(2)}) copy-start(f32[4608]{0:T(1024)} %param.17) | copy-start | bytes 55300
  47.4 11.9 %all-to-all-start.2 = ((f32[2,2,192]{1,0,2:T(2,128)}), f32[2,2,192]{1,0,2:T(2,128)S(1)}, u32[]{:S(2)}, u32[]{:S(2)}) async-start(f32[2,2,192]{1,0,2:T(2,128)} %copy.111), calls=%async_computation.2 | async-start | bytes 393216 | tf_op jit(solution)/shard_map/all_to_all | solution.py:113
  61.7 6.5 %collective-permute-start.1 = (bf16[1152,64]{0,1:T(8,128)(2,1)S(1)}, bf16[1152,64]{0,1:T(8,128)(2,1)S(1)}, u32[]{:S(2)}, u32[]{:S(2)}) collective-permute-start(bf16[1152,64]{0,1:T(8,128)(2,1)S(1)} %fusion.22), channel_id=1, source_target_pairs={{1,0},{2,1},{3,2},{4,3},{5,4},{6,5},{7,6},{8,7},{9,8},{10,9},{11,1... | collective-permute-start | bytes 442376 | tf_op jit(solution)/shard_map/ppermute | solution.py:24
  64.0 5.7 %collective-permute-start = (bf16[1152,64]{0,1:T(8,128)(2,1)S(1)}, bf16[1152,64]{0,1:T(8,128)(2,1)S(1)}, u32[]{:S(2)}, u32[]{:S(2)}) collective-permute-start(bf16[1152,64]{0,1:T(8,128)(2,1)S(1)} %fusion.21), channel_id=1, source_target_pairs={{0,1},{1,2},{2,3},{3,4},{4,5},{5,6},{6,7},{7,8},{8,9},{9,10},{10,1... | collective-permute-start | bytes 442376 | tf_op jit(solution)/shard_map/ppermute | solution.py:24
where the time goes:
time: 130 us; the launch traced here: 128 us
  local copies, waits for them, and re-layouts  51.1 us (39%)
  starting transfers between devices  18.2 us (14%)
  waiting for transfers between devices  17.1 us (13%)
  matrix products  17.1 us (13%)
  blocking collectives  13 us (10%)
  other arithmetic  9.78 us (8%)
    gather x4, local copies, waits for them, and re-layouts, one_block(): second = jnp.take(flat, second_ids, axis=0).astype(jnp.float32)  17.2 us
    gather x4, local copies, waits for them, and re-layouts, one_block(): first = jnp.take(flat, first_ids, axis=0).astype(jnp.float32)  17.2 us
    dot_general x4, matrix products, one_block(): jnp.dot(onehot, products, preferred_element_type=jnp.float32)  16.7 us
    all_to_all x1, waiting for transfers between devices, per_device(): lax.all_to_all(routed.astype(jnp.bfloat16), ('space', 'bins'), split_axis...  8.17 us
    all_to_all x1, waiting for transfers between devices, per_device(): lax.all_to_all(surface, ('space', 'bins'), split_axis=2, concat_axis=1, t...  7.01 us
    all_gather x1, blocking collectives, per_device(): lax.all_gather(group_speed.astype(jnp.bfloat16), 'bins', axis=1, tiled=True)  7 us
    unnamed x47, local copies, waits for them, and re-layouts  6.74 us
    all_gather x1, blocking collectives, per_device(): lax.all_gather(stokes_kernel.astype(jnp.float32).astype(jnp.bfloat16), 'b...  6.04 us
  transfers between devices with their start and end apart: 5, of which 4 were waited for; matrix products, arithmetic and copies ran while one was open for 9% of the time, Pallas kernels for 0%

commit v1 on v0

v1 whole, which is shorter than its diff:
```python
import functools
import jax
import jax.numpy as jnp
from jax import lax
from jax.experimental import pallas as pl
from jax.experimental.pallas import tpu as pltpu
from jax.sharding import PartitionSpec as P

DT_OCEAN = 0.5
CORIOLIS = 0.8
MIXING = 0.4
CURRENT_SCALE = 0.15
DT_SOURCE = 0.5


def shifted(value, axis, steps):
    count = lax.axis_size(axis)
    first, last = (max(0, -steps), min(count, count - steps))
    return lax.ppermute(value, axis, [(source, source + steps) for source in range(first, last)])


def levels_laplacian(field):
    upper = jnp.concatenate([field[..., :1], field[..., :-1]], axis=-1)
    lower = jnp.concatenate([field[..., 1:], field[..., -1:]], axis=-1)
    return upper + lower - 2.0 * field


def ocean_step(currents, drift, wet, levels):
    east = currents[..., :levels]
    north = currents[..., levels:]
    east_drift = drift[..., :levels]
    north_drift = drift[..., levels:]
    new_east = east + DT_OCEAN * (
        CORIOLIS * (north + north_drift) + MIXING * levels_laplacian(east)
    )
    new_north = north + DT_OCEAN * (
        -CORIOLIS * (east + east_drift) + MIXING * levels_laplacian(north)
    )
    return wet[..., None].astype(jnp.float32) * jnp.concatenate([new_east, new_north], axis=-1)


def advect_block(ext, speed_x, speed_y, cur, wet, columns):
    width = ext.shape[1] - 2 * columns
    energy = ext.astype(jnp.float32)
    cx = speed_x + cur[0:1, :]
    plus_x = jnp.maximum(cx, 0.0) * energy
    minus_x = jnp.minimum(cx, 0.0) * energy
    mid = slice(columns, columns + width)
    moved = energy[:, mid] - plus_x[:, mid] + plus_x[:, :width]
    moved = moved - minus_x[:, 2 * columns :] + minus_x[:, mid]
    cy = speed_y + cur[1:2, :]
    plus_y = jnp.maximum(cy, 0.0) * energy
    minus_y = jnp.minimum(cy, 0.0) * energy
    y = lax.rem(lax.broadcasted_iota(jnp.int32, (1, width), 1), columns)
    plus_prev = jnp.where(y == 0, 0.0, plus_y[:, columns - 1 : columns - 1 + width])
    minus_next = jnp.where(y == columns - 1, 0.0, minus_y[:, columns + 1 : columns + 1 + width])
    moved = moved - plus_y[:, mid] + plus_prev - minus_next + minus_y[:, mid]
    return (wet * moved).astype(jnp.bfloat16)


def wave_kernel(columns, chunk, ext_ref, speeds_ref, cur_ref, wet_ref, ids_ref, coef_ref, out_ref, adv, adv_t, total):
    step = pl.program_id(0)
    bins = adv.shape[0]

    @pl.when(step == 0)
    def _():
        cur = cur_ref[...]
        wet = wet_ref[...]

        def one(i, carry):
            rows = pl.ds(pl.multiple_of(i * chunk, chunk), chunk)
            speeds = speeds_ref[rows, :]
            adv[rows, :] = advect_block(
                ext_ref[rows, :], speeds[:, 0:1], speeds[:, 1:2], cur, wet, columns
            )
            return carry

        lax.fori_loop(0, bins // chunk, one, 0)
        adv_t[...] = adv[...].T
        total[...] = jnp.zeros_like(total)

    block = ids_ref.shape[1]
    bin_ids = lax.broadcasted_iota(jnp.int32, (bins, block), 0)

    def onehot(which):
        return jnp.where(bin_ids == ids_ref[which : which + 1, :], 1.0, 0.0).astype(jnp.bfloat16)

    first = jnp.dot(adv_t[...], onehot(0), preferred_element_type=jnp.float32)
    second = jnp.dot(adv_t[...], onehot(1), preferred_element_type=jnp.float32)
    products = (coef_ref[...] * first * second).astype(jnp.bfloat16)
    total[...] += lax.dot_general(
        onehot(2), products, (((1,), (1,)), ((), ())), preferred_element_type=jnp.float32
    )

    @pl.when(step == pl.num_programs(0) - 1)
    def _():
        out_ref[...] = (adv[...].astype(jnp.float32) + DT_SOURCE * total[...]).astype(jnp.bfloat16)


def wave_step(ext, speeds, cur, wet, pair_bins, pair_coef, columns):
    bins, wide = ext.shape
    width = wide - 2 * columns
    pairs = pair_bins.shape[1]
    block = 512 if pairs % 512 == 0 else pairs
    whole = lambda shape: pl.BlockSpec(shape, lambda i: (0, 0))
    chunk = 32 if bins % 32 == 0 else bins
    return pl.pallas_call(
        functools.partial(wave_kernel, columns, chunk),
        grid=(pairs // block,),
        out_shape=jax.ShapeDtypeStruct((bins, width), jnp.bfloat16),
        in_specs=[
            whole((bins, wide)),
            whole((bins, 2)),
            whole((2, wide)),
            whole((1, width)),
            pl.BlockSpec((3, block), lambda i: (0, i)),
            pl.BlockSpec((1, block), lambda i: (0, i)),
        ],
        out_specs=whole((bins, width)),
        scratch_shapes=[
            pltpu.VMEM((bins, width), jnp.bfloat16),
            pltpu.VMEM((width, bins), jnp.bfloat16),
            pltpu.VMEM((bins, width), jnp.float32),
        ],
        compiler_params=pltpu.CompilerParams(vmem_limit_bytes=48 * 1024 * 1024),
        cost_estimate=pl.CostEstimate(
            flops=6 * pairs * bins * width, bytes_accessed=4 * bins * wide, transcendentals=0
        ),
        name="wave_step",
    )(ext, speeds, cur, wet, pair_bins, pair_coef[None, :])


def per_device(
    spectrum,
    group_speed,
    stokes_kernel,
    pair_bins,
    pair_coef,
    currents,
    col_map,
    wave_wet,
    ocean_wet,
):
    local_bins, tile_rows, columns = spectrum.shape
    space_count = lax.axis_size("space")
    bins_count = lax.axis_size("bins")
    groups = space_count * bins_count
    group_cols = columns // groups
    levels = stokes_kernel.shape[1] // 2
    block_rows = tile_rows // bins_count
    width = block_rows * columns
    me = lax.axis_index("space") * bins_count + lax.axis_index("bins")
    slot_col = (
        col_map[:, None] * group_cols + jnp.arange(group_cols, dtype=jnp.int32)[None, :]
    ).reshape(-1)

    wet_f = ocean_wet.astype(jnp.float32)
    u0, u1 = currents[:, :, 0], currents[:, :, 1]
    v0, v1 = currents[:, :, levels], currents[:, :, levels + 1]
    su = wet_f * (u0 + DT_OCEAN * (CORIOLIS * v0 + MIXING * (u1 - u0)))
    sv = wet_f * (v0 + DT_OCEAN * (-CORIOLIS * u0 + MIXING * (v1 - v0)))
    surface = lax.all_gather(
        jnp.stack([su, sv, wet_f], axis=1), ("space", "bins"), axis=0, tiled=True
    )

    sending = jnp.transpose(spectrum.reshape(local_bins, bins_count, width), (1, 0, 2))
    flat = lax.all_to_all(sending, "bins", split_axis=0, concat_axis=0, tiled=True)
    flat = flat.reshape(bins_count * local_bins, width)
    below = shifted(flat[:, width - columns :], ("space", "bins"), 1)
    above = shifted(flat[:, :columns], ("space", "bins"), -1)
    ext = jnp.concatenate([below, flat, above], axis=1)

    speed_hi = group_speed.astype(jnp.bfloat16)
    speed_lo = (group_speed - speed_hi.astype(jnp.float32)).astype(jnp.bfloat16)
    tables = jnp.concatenate([stokes_kernel, speed_hi.T, speed_lo.T], axis=1)
    tables = lax.all_gather(tables, "bins", axis=0, tiled=True)
    kernel_all = tables[:, : 2 * levels]
    speeds = tables[:, 2 * levels :].astype(jnp.float32)
    speeds = speeds[:, 0:2] + speeds[:, 2:4]

    drift_cells = lax.dot_general(
        ext, kernel_all, (((0,), (0,)), ((), ())), preferred_element_type=jnp.float32
    )
    padded = jnp.pad(surface, ((0, 0), (0, 0), (1, 1)))
    mine = lax.dynamic_slice_in_dim(padded, me * block_rows, block_rows + 2, 2)
    here = slot_col[:, None] == jnp.arange(columns, dtype=jnp.int32)[None, :]
    mine = jnp.sum(jnp.where(here[:, None, None, :], mine[:, :, :, None], 0.0), axis=0)
    mine = mine.reshape(3, (block_rows + 2) * columns)
    half = DT_OCEAN * CORIOLIS
    cur = CURRENT_SCALE * jnp.tanh(
        jnp.stack(
            [
                mine[0] + half * mine[2] * drift_cells[:, levels],
                mine[1] - half * mine[2] * drift_cells[:, 0],
            ]
        )
    )
    wet_rows = lax.dynamic_slice_in_dim(
        wave_wet, lax.axis_index("bins") * block_rows, block_rows, 0
    )
    wet_rows = wet_rows.astype(jnp.float32).reshape(1, width)

    inner = drift_cells[columns : columns + width].reshape(block_rows, columns, 2 * levels)
    routed = jnp.einsum(
        "jc,xcl->jxl",
        here.astype(jnp.bfloat16),
        inner.astype(jnp.bfloat16),
        preferred_element_type=jnp.float32,
    ).astype(jnp.bfloat16)
    drift = lax.all_to_all(
        routed, ("space", "bins"), split_axis=0, concat_axis=1, tiled=True
    ).astype(jnp.float32)
    new_currents = ocean_step(currents, drift, ocean_wet, levels)

    updated = wave_step(ext, speeds, cur, wet_rows, pair_bins, pair_coef, columns)
    new_spectrum = updated.reshape(bins_count * local_bins, block_rows, columns)
    return (new_spectrum, new_currents)


def solution(mesh):
    placed = (
        P("bins", "space", None),
        P(None, "bins"),
        P("bins", None),
        P(),
        P(),
        P(("space", "bins"), None, None),
        P(),
        P("space", None),
        P(("space", "bins"), None),
    )
    return jax.shard_map(
        per_device,
        mesh=mesh,
        in_specs=placed,
        out_specs=(P(None, ("space", "bins"), None), P(("space", "bins"), None, None)),
        check_vma=False,
    )
```

time: 130 us -> 116 us (0.89); the launches traced: 128 us -> 116 us
  blocking collectives: 13 us -> 52.6 us
  local copies, waits for them, and re-layouts: 51.1 us -> 13.4 us
  Pallas kernels: 0 us -> 29.6 us
  matrix products: 17.1 us -> 0.6 us
  waiting for transfers between devices: 17.1 us -> 3.53 us
  other arithmetic: 9.78 us -> 3.36 us
  starting transfers between devices: 18.2 us -> 11.8 us
    all_gather x2, blocking collectives: 13 us -> 52.6 us  [the longest x1 45.9 us: per_device(): lax.all_gather(jnp.stack([su, sv, wet_f], axis=1), ('space', 'bins'), axi...]
    gather x10 -> x0, local copies, waits for them, and re-layouts: 35.9 us -> none  [the longest x4 17.2 us: one_block(): second = jnp.take(flat, second_ids, axis=0).astype(jnp.float32)]
    pallas_call x0 -> x1, Pallas kernels: none -> 29.6 us  [wave_step(): pl.pallas_call(functools.partial(wave_kernel, columns, chunk), grid=(pair...]
    dot_general x4 -> x2, matrix products: 16.7 us -> 0.6 us  [the longest x1 0.37 us: per_device(): lax.dot_general(ext, kernel_all, (((0,), (0,)), ((), ())), preferred_elem...]
    all_to_all x3 -> x2, waiting for transfers between devices: 15.2 us -> 0.01 us  [the longest x1 0.01 us: per_device(): lax.all_to_all(sending, 'bins', split_axis=0, concat_axis=0, tiled=True)]
    all_to_all x3 -> x2, starting transfers between devices: 12.4 us -> 6.72 us  [the longest x1 4.42 us: per_device(): lax.all_to_all(sending, 'bins', split_axis=0, concat_axis=0, tiled=True)]
    convert_element_type x8 -> x3, other arithmetic: 5.86 us -> 0.76 us  [the longest x1 0.71 us: per_device(): wet_rows = wet_rows.astype(jnp.float32).reshape(1, width)]
    all_to_all x5 -> x0, local copies, waits for them, and re-layouts: 2.29 us -> none  [the longest x2 1.66 us: per_device(): lax.all_to_all(spectrum, 'bins', split_axis=1, concat_axis=0, tiled=True)]
  transfers between devices with their start and end apart: 5 -> 4, of which waited for: 4 -> 1; matrix products, arithmetic and copies ran while one was open for 9% -> 8% of each run, Pallas kernels for 0% -> 26%
where the time goes in v1:
time: 116 us
  blocking collectives  52.6 us (45%)
  Pallas kernels  29.6 us (26%)
  local copies, waits for them, and re-layouts  13.4 us (12%)
  starting transfers between devices  11.8 us (10%)
  waiting for transfers between devices  3.53 us (3%)
  other arithmetic  3.36 us (3%)
    all_gather x1, blocking collectives, per_device(): lax.all_gather(jnp.stack([su, sv, wet_f], axis=1), ('space', 'bins'), axi...  45.9 us
    pallas_call x1, Pallas kernels, wave_step(): pl.pallas_call(functools.partial(wave_kernel, columns, chunk), grid=(pair...  29.6 us
    all_gather x1, blocking collectives, per_device(): tables = lax.all_gather(tables, 'bins', axis=0, tiled=True)  6.71 us
    unnamed x42, local copies, waits for them, and re-layouts  6.71 us
    ppermute x2, starting transfers between devices, shifted(): lax.ppermute(value, axis, [(source, source + steps) for source in range(f...  5.04 us
    all_to_all x1, starting transfers between devices, per_device(): lax.all_to_all(sending, 'bins', split_axis=0, concat_axis=0, tiled=True)  4.42 us
    ppermute x2, waiting for transfers between devices, shifted(): lax.ppermute(value, axis, [(source, source + steps) for source in range(f...  3.52 us
  transfers between devices with their start and end apart: 4, of which 1 were waited for; matrix products, arithmetic and copies ran while one was open for 8% of the time, Pallas kernels for 26%

profile of v1, /device:TPU:1, one launch (start us, length us, event | category | flops | bytes accessed | tf_op | source)
XLA Modules:
  0.0 115.8 jit_solution(18395480726521931756)
XLA Ops:
  0.6 2.3 %copy.93 = bf16[288,4,384]{2,0,1:T(8,128)(2,1)} copy(bf16[288,4,384]{0,2,1:T(8,128)(2,1)} %bitcast.93) | data formatting | bytes 1769472 | tf_op jit(solution)/shard_map/reshape | solution.py:166
  2.9 4.4 %all-to-all-start = ((bf16[4,288,384]{2,1,0:T(8,128)(2,1)}), bf16[4,288,384]{2,1,0:T(8,128)(2,1)S(1)}, u32[]{:S(2)}, u32[]{:S(2)}) async-start(bf16[4,288,384]{2,1,0:T(8,128)(2,1)} %bitcast.1), calls=%async_computation | async-start | bytes 1769472 | tf_op jit(solution)/shard_map/all_to_all | solution.py:167
  7.3 0.3 fusion.33
  7.7 0.1 copy.116
  7.8 0.1 copy.118
  7.9 0.1 copy.117
  8.0 0.1 copy.119
  8.2 0.1 copy.120
  8.3 0.1 copy.121
  8.5 45.9 %all_gather.7 = f32[64,3,192]{2,1,0:T(4,128)S(1)} all-gather(f32[2,3,192]{2,1,0:T(4,128)S(1)} %copy.100), channel_id=1, replica_groups=mesh['space'=8,'bins'=4] {'space','bins'}, dimensions={0}, use_global_device_ids=true | all-gather | bytes 152064 | tf_op jit(solution)/shard_map/all_gather | solution.py:162
  54.4 0.1 add.84
  54.6 0.1 pad_dynamic-slice_fusion
  54.7 0.3 select_reduce_fusion
  55.3 0.1 copy.94
  55.5 6.7 %all-gather = bf16[4,288,132]{1,2,0:T(8,128)(2,1)S(1)} all-gather(bf16[1,288,132]{1,2,0:T(8,128)(2,1)S(1)} %maximum_bitcast_fusion), channel_id=1, replica_groups=mesh['space'=8,'bins'=4] {'bins'}, dimensions={0}, use_global_device_ids=true | all-gather | bytes 380160 | tf_op jit(solution)/shard_map/all_gather | solution.py:176
  62.2 0.3 copy.95
  62.4 0.7 dynamic-slice_convert_fusion
  63.2 0.1 reshape.123.wet_ref
  63.3 0.1 copy.127
  63.4 0.1 copy.131
  63.5 0.2 fusion.32
  63.8 0.1 copy.125
  63.9 0.8 copy.126
  64.7 0.8 copy.129
  65.5 0.8 copy.130
  66.3 0.2 slice_add_fusion.speeds_ref
  66.5 0.2 fusion.30
  66.6 2.1 %collective-permute-start = (bf16[1152,64]{1,0:T(8,128)(2,1)S(1)}, bf16[1152,64]{1,0:T(8,128)(2,1)}, u32[]{:S(2)}, u32[]{:S(2)}) collective-permute-start(bf16[1152,64]{1,0:T(8,128)(2,1)S(1)} %get-tuple-element.12), channel_id=1, source_target_pairs={{0,1},{1,2},{2,3},{3,4},{4,5},{5,6},{6,7},{7,8},{8,9},{9,10},{10,1... | collective-permute-start | bytes 442376 | tf_op jit(solution)/shard_map/ppermute | solution.py:19
  68.7 2.9 %collective-permute-start.1 = (bf16[1152,64]{1,0:T(8,128)(2,1)S(1)}, bf16[1152,64]{1,0:T(8,128)(2,1)}, u32[]{:S(2)}, u32[]{:S(2)}) collective-permute-start(bf16[1152,64]{1,0:T(8,128)(2,1)S(1)} %get-tuple-element.13), channel_id=1, source_target_pairs={{1,0},{2,1},{3,2},{4,3},{5,4},{6,5},{7,6},{8,7},{9,8},{10,9},{11,1... | collective-permute-start | bytes 442376 | tf_op jit(solution)/shard_map/ppermute | solution.py:19
  71.7 0.1 fusion.34
  71.8 0.8 copy.122
  72.6 0.8 copy.123
  73.4 3.5 %collective-permute-done.1 = bf16[1152,64]{1,0:T(8,128)(2,1)} collective-permute-done((bf16[1152,64]{1,0:T(8,128)(2,1)S(1)}, bf16[1152,64]{1,0:T(8,128)(2,1)}, u32[]{:S(2)}, u32[]{:S(2)}) %collective-permute-start.1) | collective-permute-done | bytes 147488 | tf_op jit(solution)/shard_map/ppermute | solution.py:19
  76.9 1.7 %pad_maximum_fusion.ext_ref = bf16[1152,512]{1,0:T(8,128)(2,1)S(1)} fusion(bf16[1152,64]{1,0:T(8,128)(2,1)} %collective-permute-done.1, bf16[1152,384]{1,0:T(8,128)(2,1)S(1)} %bitcast.89, bf16[1152,64]{1,0:T(8,128)(2,1)} %collective-permute-done), kind=kLoop, calls=%fused_computation | loop fusion | flops 3538944 | bytes 2359296 | tf_op jit(solution)/shard_map/concatenate | solution.py:171
  78.7 0.4 fusion
  79.0 0.1 slice.150
  79.1 0.1 copy.104
  79.3 0.2 convolution_convert_fusion
  79.5 0.7 copy.105
  80.2 2.3 %all-to-all-start.1 = ((bf16[64,6,128]{2,1,0:T(8,128)(2,1)}), bf16[64,6,128]{2,1,0:T(8,128)(2,1)S(1)}, u32[]{:S(2)}, u32[]{:S(2)}) async-start(bf16[64,6,128]{2,1,0:T(8,128)(2,1)} %copy.105), calls=%async_computation.1 | async-start | bytes 262144 | tf_op jit(solution)/shard_map/all_to_all | solution.py:210
  82.6 29.6 %wave_step.1 = bf16[1152,384]{1,0:T(8,128)(2,1)S(1)} custom-call(bf16[1152,512]{1,0:T(8,128)(2,1)S(1)} %pad_maximum_fusion.ext_ref, f32[1152,2]{1,0:T(8,128)S(1)} %slice_add_fusion.speeds_ref, f32[2,512]{1,0:T(2,128)S(1)} %fusion.13.cur_ref, f32[1,384]{1,0:T(1,128)S(1)} %reshape.123.wet_ref, s32[3,4608]{1,0:T(4,128)S(1)} %copy-done, ...), custom_call_target="tpu_custom_call" | custom-call | flops 12230590464 | bytes 2359296 | tf_op jit(solution)/shard_map/wave_step/pallas_call | solution.py:107
  112.1 1.5 %copy.101 = bf16[1152,384]{0,1:T(8,128)(2,1)} copy(bf16[1152,384]{1,0:T(8,128)(2,1)S(1)} %wave_step.1) | data formatting | bytes 1769472 | tf_op jit(solution)/shard_map/wave_step/pallas_call | solution.py:107
  113.8 0.3 fusion.31
  114.0 0.1 copy.124
  114.2 0.1 copy.128
  114.3 0.3 copy-done.2
  114.8 0.1 fusion.6
  115.0 0.8 copy.115
  (45 shorter events, 0.9 us)
Async XLA Ops:
  2.9 4.4 %copy-start.1 = (f32[2,192,128]{2,1,0:T(8,128)S(1)}, f32[2,192,128]{2,1,0:T(8,128)}, u32[]{:S(2)}) copy-start(f32[2,192,128]{2,1,0:T(8,128)} %param.14) | copy-start | bytes 589828
  2.9 63.6 %all-to-all-start = ((bf16[4,288,384]{2,1,0:T(8,128)(2,1)}), bf16[4,288,384]{2,1,0:T(8,128)(2,1)S(1)}, u32[]{:S(2)}, u32[]{:S(2)}) async-start(bf16[4,288,384]{2,1,0:T(8,128)(2,1)} %bitcast.1), calls=%async_computation | async-start | bytes 1769472 | tf_op jit(solution)/shard_map/all_to_all | solution.py:167
  7.6 0.8 copy-start.9
  7.7 46.7 %copy-start.11 = (s32[32]{0:T(128)S(1)}, s32[32]{0:T(128)}, u32[]{:S(2)}) copy-start(s32[32]{0:T(128)} %param.15) | copy-start | bytes 388
  7.7 47.6 %copy-start.10 = (f32[2,288]{1,0:T(2,128)S(1)}, f32[2,288]{1,0:T(2,128)}, u32[]{:S(2)}) copy-start(f32[2,288]{1,0:T(2,128)} %param.10) | copy-start | bytes 6916
  7.7 47.6 %copy-start.7 = (bf16[288,128]{1,0:T(8,128)(2,1)S(1)}, bf16[288,128]{1,0:T(8,128)(2,1)}, u32[]{:S(2)}) copy-start(bf16[288,128]{1,0:T(8,128)(2,1)} %param.11) | copy-start | bytes 221188
  55.4 7.8 %copy-start.8 = (f32[4608]{0:T(1024)S(1)}, f32[4608]{0:T(1024)}, u32[]{:S(2)}) copy-start(f32[4608]{0:T(1024)} %param.13) | copy-start | bytes 55300
  66.6 6.7 %collective-permute-start = (bf16[1152,64]{1,0:T(8,128)(2,1)S(1)}, bf16[1152,64]{1,0:T(8,128)(2,1)}, u32[]{:S(2)}, u32[]{:S(2)}) collective-permute-start(bf16[1152,64]{1,0:T(8,128)(2,1)S(1)} %get-tuple-element.12), channel_id=1, source_target_pairs={{0,1},{1,2},{2,3},{3,4},{4,5},{5,6},{6,7},{7,8},{8,9},{9,10},{10,1... | collective-permute-start | bytes 442376 | tf_op jit(solution)/shard_map/ppermute | solution.py:19
  68.7 8.1 %collective-permute-start.1 = (bf16[1152,64]{1,0:T(8,128)(2,1)S(1)}, bf16[1152,64]{1,0:T(8,128)(2,1)}, u32[]{:S(2)}, u32[]{:S(2)}) collective-permute-start(bf16[1152,64]{1,0:T(8,128)(2,1)S(1)} %get-tuple-element.13), channel_id=1, source_target_pairs={{1,0},{2,1},{3,2},{4,3},{5,4},{6,5},{7,6},{8,7},{9,8},{10,9},{11,1... | collective-permute-start | bytes 442376 | tf_op jit(solution)/shard_map/ppermute | solution.py:19
  78.6 3.9 %copy-start = (s32[3,4608]{1,0:T(4,128)S(1)}, s32[3,4608]{1,0:T(4,128)}, u32[]{:S(2)}) copy-start(s32[3,4608]{1,0:T(4,128)} %ids_ref.1) | copy-start | bytes 165892
  80.2 33.4 %all-to-all-start.1 = ((bf16[64,6,128]{2,1,0:T(8,128)(2,1)}), bf16[64,6,128]{2,1,0:T(8,128)(2,1)S(1)}, u32[]{:S(2)}, u32[]{:S(2)}) async-start(bf16[64,6,128]{2,1,0:T(8,128)(2,1)} %copy.105), calls=%async_computation.1 | async-start | bytes 262144 | tf_op jit(solution)/shard_map/all_to_all | solution.py:210
  113.6 0.9 copy-start.2
  113.6 1.0 copy-start.3
  113.6 1.0 copy-start.4
  113.6 1.1 copy-start.5
  113.7 1.2 copy-start.6

commit v2 on v1

--- a/solution.py
+++ b/solution.py
@@ -13,10 +13,182 @@
 DT_SOURCE = 0.5
 
 
-def shifted(value, axis, steps):
-    count = lax.axis_size(axis)
-    first, last = (max(0, -steps), min(count, count - steps))
-    return lax.ppermute(value, axis, [(source, source + steps) for source in range(first, last)])
+def exchange_kernel(
+    space_count,
+    bins_count,
+    windows,
+    table,
+    speeds,
+    edges,
+    surface,
+    windows_out,
+    table_out,
+    speeds_out,
+    edges_out,
+    surface_out,
+    own_sem,
+    send_sem,
+    recv_sem,
+    edge_send,
+    edge_recv,
+    surface_send,
+    surface_recv,
+):
+    space, part = lax.axis_index("space"), lax.axis_index("bins")
+    total = space_count * bins_count
+    me = space * bins_count + part
+    local_bins = table.shape[0]
+    mine = pl.ds(pl.multiple_of(part * local_bins, 32), local_bins)
+
+    def place(other):
+        return (other // bins_count, lax.rem(other, bins_count))
+
+    def remote(source, target, sent, received, device):
+        return pltpu.make_async_remote_copy(
+            src_ref=source,
+            dst_ref=target,
+            send_sem=sent,
+            recv_sem=received,
+            device_id=device,
+            device_id_type=pl.DeviceIdType.MESH,
+        )
+
+    own = [
+        pltpu.make_async_copy(windows.at[part], windows_out.at[mine, :], own_sem.at[0]),
+        pltpu.make_async_copy(table, table_out.at[mine, :], own_sem.at[1]),
+        pltpu.make_async_copy(speeds, speeds_out.at[part], own_sem.at[2]),
+        pltpu.make_async_copy(surface.at[me], surface_out.at[me], own_sem.at[3]),
+    ]
+    for copy in own:
+        copy.start()
+
+    barrier = pltpu.get_barrier_semaphore()
+
+    def greet(k, carry):
+        pl.semaphore_signal(
+            barrier,
+            inc=1,
+            device_id=place(lax.rem(me + k, total)),
+            device_id_type=pl.DeviceIdType.MESH,
+        )
+        return carry
+
+    lax.fori_loop(1, total, greet, 0)
+    pl.semaphore_wait(barrier, total - 1)
+
+    sends = []
+    for j in range(1, bins_count):
+        peer = lax.rem(part + j, bins_count)
+        device = (space, peer)
+        sends.append(
+            remote(speeds, speeds_out.at[part], send_sem.at[0, j], recv_sem.at[0, j], device)
+        )
+        sends.append(
+            remote(table, table_out.at[mine, :], send_sem.at[1, j], recv_sem.at[1, j], device)
+        )
+        sends.append(
+            remote(
+                windows.at[peer],
+                windows_out.at[mine, :],
+                send_sem.at[2, j],
+                recv_sem.at[2, j],
+                device,
+            )
+        )
+    for copy in sends:
+        copy.start()
+
+    def up():
+        return remote(
+            edges.at[0],
+            edges_out.at[mine, :],
+            edge_send.at[0],
+            edge_recv.at[part],
+            (space + 1, 0),
+        )
+
+    def down():
+        return remote(
+            edges.at[1],
+            edges_out.at[mine, :],
+            edge_send.at[1],
+            edge_recv.at[part],
+            (space - 1, bins_count - 1),
+        )
+
+    pl.when(space < space_count - 1)(lambda: up().start())
+    pl.when(space > 0)(lambda: down().start())
+
+    def to_other(k):
+        other = lax.rem(me + k, total)
+        return remote(
+            surface.at[other],
+            surface_out.at[me],
+            surface_send.at[k],
+            surface_recv.at[k],
+            place(other),
+        )
+
+    def start_one(k, carry):
+        to_other(k).start()
+        return carry
+
+    def finish_one(k, carry):
+        to_other(k).wait()
+        return carry
+
+    lax.fori_loop(1, total, start_one, 0)
+    lax.fori_loop(1, total, finish_one, 0)
+    pl.when(space < space_count - 1)(lambda: up().wait_send())
+    pl.when(space > 0)(lambda: down().wait_send())
+
+    def arrive(which):
+        rows = pl.ds(which * local_bins, local_bins)
+        remote(
+            edges.at[0], edges_out.at[rows, :], edge_send.at[0], edge_recv.at[which], (space, part)
+        ).wait_recv()
+
+    def arrive_all():
+        for which in range(bins_count):
+            arrive(which)
+
+    pl.when((part == 0) & (space > 0))(arrive_all)
+    pl.when((part == bins_count - 1) & (space < space_count - 1))(arrive_all)
+    for copy in sends:
+        copy.wait()
+    for copy in own:
+        copy.wait()
+
+
+def exchange(windows, table, speeds, edges, surface, space_count, bins_count):
+    anywhere = pl.BlockSpec(memory_space=pl.ANY)
+    local_bins = table.shape[0]
+    bins = local_bins * bins_count
+    total = space_count * bins_count
+    dma = pltpu.SemaphoreType.DMA
+    return pl.pallas_call(
+        functools.partial(exchange_kernel, space_count, bins_count),
+        out_shape=(
+            jax.ShapeDtypeStruct((bins, windows.shape[2]), windows.dtype),
+            jax.ShapeDtypeStruct((bins, table.shape[1]), table.dtype),
+            jax.ShapeDtypeStruct((bins_count,) + speeds.shape, speeds.dtype),
+            jax.ShapeDtypeStruct((bins, edges.shape[2]), edges.dtype),
+            jax.ShapeDtypeStruct(surface.shape, surface.dtype),
+        ),
+        in_specs=[anywhere] * 5,
+        out_specs=(anywhere,) * 5,
+        scratch_shapes=[
+            dma((4,)),
+            dma((3, bins_count)),
+            dma((3, bins_count)),
+            dma((2,)),
+            dma((bins_count,)),
+            dma((total,)),
+            dma((total,)),
+        ],
+        compiler_params=pltpu.CompilerParams(collective_id=0, has_side_effects=True),
+        name="exchange",
+    )(windows, table, speeds, edges, surface)
 
 
 def levels_laplacian(field):
@@ -41,7 +213,7 @@
 
 def advect_block(ext, speed_x, speed_y, cur, wet, columns):
     width = ext.shape[1] - 2 * columns
-    energy = ext.astype(jnp.float32)
+    energy = ext
     cx = speed_x + cur[0:1, :]
     plus_x = jnp.maximum(cx, 0.0) * energy
     minus_x = jnp.minimum(cx, 0.0) * energy
@@ -58,7 +230,7 @@
     return (wet * moved).astype(jnp.bfloat16)
 
 
-def wave_kernel(columns, chunk, ext_ref, speeds_ref, cur_ref, wet_ref, ids_ref, coef_ref, out_ref, adv, adv_t, total):
+def wave_kernel(columns, chunk, win_ref, near_ref, speeds_ref, cur_ref, wet_ref, ids_ref, coef_ref, out_ref, adv, adv_t, total):
     step = pl.program_id(0)
     bins = adv.shape[0]
 
@@ -70,8 +242,11 @@
         def one(i, carry):
             rows = pl.ds(pl.multiple_of(i * chunk, chunk), chunk)
             speeds = speeds_ref[rows, :]
+            near = near_ref[rows, :].astype(jnp.float32)
+            main = win_ref[rows, 2 * columns :].astype(jnp.float32)
+            ext = jnp.concatenate([near[:, :columns], main, near[:, columns:]], axis=1)
             adv[rows, :] = advect_block(
-                ext_ref[rows, :], speeds[:, 0:1], speeds[:, 1:2], cur, wet, columns
+                ext, speeds[:, 0:1], speeds[:, 1:2], cur, wet, columns
             )
             return carry
 
@@ -97,8 +272,8 @@
         out_ref[...] = (adv[...].astype(jnp.float32) + DT_SOURCE * total[...]).astype(jnp.bfloat16)
 
 
-def wave_step(ext, speeds, cur, wet, pair_bins, pair_coef, columns):
-    bins, wide = ext.shape
+def wave_step(win, near, speeds, cur, wet, pair_bins, pair_coef, columns):
+    bins, wide = win.shape
     width = wide - 2 * columns
     pairs = pair_bins.shape[1]
     block = 512 if pairs % 512 == 0 else pairs
@@ -110,6 +285,7 @@
         out_shape=jax.ShapeDtypeStruct((bins, width), jnp.bfloat16),
         in_specs=[
             whole((bins, wide)),
+            whole((bins, 2 * columns)),
             whole((bins, 2)),
             whole((2, wide)),
             whole((1, width)),
@@ -127,7 +303,7 @@
             flops=6 * pairs * bins * width, bytes_accessed=4 * bins * wide, transcendentals=0
         ),
         name="wave_step",
-    )(ext, speeds, cur, wet, pair_bins, pair_coef[None, :])
+    )(win, near, speeds, cur, wet, pair_bins, pair_coef[None, :])
 
 
 def per_device(
@@ -149,7 +325,6 @@
     levels = stokes_kernel.shape[1] // 2
     block_rows = tile_rows // bins_count
     width = block_rows * columns
-    me = lax.axis_index("space") * bins_count + lax.axis_index("bins")
     slot_col = (
         col_map[:, None] * group_cols + jnp.arange(group_cols, dtype=jnp.int32)[None, :]
     ).reshape(-1)
@@ -159,39 +334,68 @@
     v0, v1 = currents[:, :, levels], currents[:, :, levels + 1]
     su = wet_f * (u0 + DT_OCEAN * (CORIOLIS * v0 + MIXING * (u1 - u0)))
     sv = wet_f * (v0 + DT_OCEAN * (-CORIOLIS * u0 + MIXING * (v1 - v0)))
-    surface = lax.all_gather(
-        jnp.stack([su, sv, wet_f], axis=1), ("space", "bins"), axis=0, tiled=True
-    )
-
-    sending = jnp.transpose(spectrum.reshape(local_bins, bins_count, width), (1, 0, 2))
-    flat = lax.all_to_all(sending, "bins", split_axis=0, concat_axis=0, tiled=True)
-    flat = flat.reshape(bins_count * local_bins, width)
-    below = shifted(flat[:, width - columns :], ("space", "bins"), 1)
-    above = shifted(flat[:, :columns], ("space", "bins"), -1)
-    ext = jnp.concatenate([below, flat, above], axis=1)
-
-    speed_hi = group_speed.astype(jnp.bfloat16)
-    speed_lo = (group_speed - speed_hi.astype(jnp.float32)).astype(jnp.bfloat16)
-    tables = jnp.concatenate([stokes_kernel, speed_hi.T, speed_lo.T], axis=1)
-    tables = lax.all_gather(tables, "bins", axis=0, tiled=True)
-    kernel_all = tables[:, : 2 * levels]
-    speeds = tables[:, 2 * levels :].astype(jnp.float32)
-    speeds = speeds[:, 0:2] + speeds[:, 2:4]
-
-    drift_cells = lax.dot_general(
-        ext, kernel_all, (((0,), (0,)), ((), ())), preferred_element_type=jnp.float32
-    )
-    padded = jnp.pad(surface, ((0, 0), (0, 0), (1, 1)))
-    mine = lax.dynamic_slice_in_dim(padded, me * block_rows, block_rows + 2, 2)
+    surface = jnp.stack([su, sv, wet_f])
+
+    def windows_of(rows, before, after):
+        before = jnp.concatenate([before, rows[..., :-1, -1:]], axis=-2)
+        after = jnp.concatenate([rows[..., 1:, :1], after], axis=-2)
+        return jnp.concatenate([before, after, rows], axis=-1)
+
+    none = jnp.zeros((3, group_cols, 1, 1), jnp.float32)
+    surface = windows_of(
+        surface.reshape(3, group_cols, groups, block_rows), none, none
+    )
+    window_rows = block_rows + 2
+    surface = jnp.transpose(surface, (2, 0, 1, 3)).reshape(groups, 1, 3 * group_cols * window_rows)
+    used = surface.shape[2]
+    surface = jnp.pad(surface, ((0, 0), (0, 0), (0, -used % 128)))
+
+    rows = spectrum.reshape(local_bins, bins_count, width)
+    zeros = jnp.zeros((local_bins, 1, columns), spectrum.dtype)
+    before = jnp.concatenate([zeros, rows[:, :-1, width - columns :]], axis=1)
+    after = jnp.concatenate([rows[:, 1:, :columns], zeros], axis=1)
+    windows = jnp.transpose(jnp.concatenate([before, after, rows], axis=2), (1, 0, 2))
+    zero = zeros[:, 0]
+    edges = jnp.stack(
+        [
+            jnp.concatenate([spectrum[:, -1, :], zero], axis=1),
+            jnp.concatenate([zero, spectrum[:, 0, :]], axis=1),
+        ]
+    )
+    speeds = jnp.pad(group_speed, ((0, -2 % 8), (0, -local_bins % 128)))
+    win, kernel_all, speeds, edges, surface = exchange(
+        windows, stokes_kernel, speeds, edges, surface, space_count, bins_count
+    )
+    speeds = jnp.transpose(speeds[:, :2, :local_bins], (0, 2, 1)).reshape(-1, 2)
+    space, part = lax.axis_index("space"), lax.axis_index("bins")
+    from_below = (part == 0) & (space > 0)
+    from_above = (part == bins_count - 1) & (space < space_count - 1)
+    is_below = jnp.arange(2 * columns, dtype=jnp.int32) < columns
+    take_edge = jnp.where(is_below, from_below, from_above)
+    near = jnp.where(take_edge[None, :], edges, win[:, : 2 * columns])
+
+    def project(cells):
+        return lax.dot_general(
+            cells, kernel_all, (((0,), (0,)), ((), ())), preferred_element_type=jnp.float32
+        )
+
+    drift_near, drift_main = project(near), project(win[:, 2 * columns :])
+
+    def in_order(cells_near, cells_main):
+        return jnp.concatenate([cells_near[:columns], cells_main, cells_near[columns:]])
+
+    mine = surface[:, 0, :used].reshape(groups, 3, group_cols, window_rows)
+    mine = jnp.transpose(mine, (0, 2, 1, 3)).reshape(groups * group_cols, 3, window_rows)
     here = slot_col[:, None] == jnp.arange(columns, dtype=jnp.int32)[None, :]
     mine = jnp.sum(jnp.where(here[:, None, None, :], mine[:, :, :, None], 0.0), axis=0)
-    mine = mine.reshape(3, (block_rows + 2) * columns)
+    mine = jnp.concatenate([mine[:, :1], mine[:, 2:], mine[:, 1:2]], axis=1)
+    mine = mine.reshape(3, window_rows * columns)
     half = DT_OCEAN * CORIOLIS
     cur = CURRENT_SCALE * jnp.tanh(
         jnp.stack(
             [
-                mine[0] + half * mine[2] * drift_cells[:, levels],
-                mine[1] - half * mine[2] * drift_cells[:, 0],
+                mine[0] + half * mine[2] * in_order(drift_near[:, levels], drift_main[:, levels]),
+                mine[1] - half * mine[2] * in_order(drift_near[:, 0], drift_main[:, 0]),
             ]
         )
     )
@@ -200,7 +404,7 @@
     )
     wet_rows = wet_rows.astype(jnp.float32).reshape(1, width)
 
-    inner = drift_cells[columns : columns + width].reshape(block_rows, columns, 2 * levels)
+    inner = drift_main.reshape(block_rows, columns, 2 * levels)
     routed = jnp.einsum(
         "jc,xcl->jxl",
         here.astype(jnp.bfloat16),
@@ -212,7 +416,7 @@
     ).astype(jnp.float32)
     new_currents = ocean_step(currents, drift, ocean_wet, levels)
 
-    updated = wave_step(ext, speeds, cur, wet_rows, pair_bins, pair_coef, columns)
+    updated = wave_step(win, near, speeds, cur, wet_rows, pair_bins, pair_coef, columns)
     new_spectrum = updated.reshape(bins_count * local_bins, block_rows, columns)
     return (new_spectrum, new_currents)
 

time: 116 us -> 84.2 us (0.73)
  blocking collectives: 52.6 us -> 0 us
  Pallas kernels: 29.6 us -> 56.3 us
  starting transfers between devices: 11.8 us -> 3.45 us
  waiting for transfers between devices: 3.53 us -> 0.01 us
  local copies, waits for them, and re-layouts: 13.4 us -> 16.3 us
  matrix products: 0.6 us -> 2.86 us
    all_gather x2 -> x0, blocking collectives: 52.6 us -> none  [the longest x1 45.9 us: per_device(): lax.all_gather(jnp.stack([su, sv, wet_f], axis=1), ('space', 'bins'), axi...]
    pallas_call x0 -> x1, Pallas kernels: none -> 26.5 us  [exchange(): pl.pallas_call(functools.partial(exchange_kernel, space_count, bins_count...]
    ppermute x2 -> x0, starting transfers between devices: 5.04 us -> none  [shifted(): lax.ppermute(value, axis, [(source, source + steps) for source in range(f...]
    all_to_all x1 -> x0, starting transfers between devices: 4.42 us -> none  [per_device(): lax.all_to_all(sending, 'bins', split_axis=0, concat_axis=0, tiled=True)]
    ppermute x2 -> x0, waiting for transfers between devices: 3.52 us -> none  [shifted(): lax.ppermute(value, axis, [(source, source + steps) for source in range(f...]
    dot_general x1 -> x2, matrix products: 0.37 us -> 2.64 us  [project(): lax.dot_general(cells, kernel_all, (((0,), (0,)), ((), ())), preferred_el...]
    slice x2, local copies, waits for them, and re-layouts: 0.55 us -> 2.68 us  [levels_laplacian(): lower = jnp.concatenate([field[..., 1:], field[..., -1:]], axis=-1)]
    unnamed x42 -> x51, local copies, waits for them, and re-layouts: 6.71 us -> 4.62 us
  transfers between devices with their start and end apart: 4 -> 1, of which waited for: 1 -> 0; matrix products, arithmetic and copies ran while one was open for 8% -> 10% of each run, Pallas kernels for 26% -> 36%
where the time goes in v2:
time: 84.2 us; the launch traced here: 83.4 us
  Pallas kernels  56.3 us (67%)
  local copies, waits for them, and re-layouts  16.3 us (19%)
  other arithmetic  3.45 us (4%)
  starting transfers between devices  3.45 us (4%)
  matrix products  2.86 us (3%)
  between operations  1.03 us (1%)
    pallas_call x1, Pallas kernels, wave_step(): pl.pallas_call(functools.partial(wave_kernel, columns, chunk), grid=(pair...  29.7 us
    pallas_call x1, Pallas kernels, exchange(): pl.pallas_call(functools.partial(exchange_kernel, space_count, bins_count...  26.5 us
    unnamed x51, local copies, waits for them, and re-layouts  4.62 us
    all_to_all x1, starting transfers between devices, per_device(): lax.all_to_all(routed, ('space', 'bins'), split_axis=0, concat_axis=1, ti...  3.45 us
    slice x2, local copies, waits for them, and re-layouts, levels_laplacian(): lower = jnp.concatenate([field[..., 1:], field[..., -1:]], axis=-1)  2.68 us
    dot_general x2, matrix products, project(): lax.dot_general(cells, kernel_all, (((0,), (0,)), ((), ())), preferred_el...  2.64 us
  transfers between devices with their start and end apart: 1, of which 0 were waited for; matrix products, arithmetic and copies ran while one was open for 10% of the time, Pallas kernels for 36%

profile of v2, /device:TPU:1, one launch (start us, length us, event | category | flops | bytes accessed | tf_op | source)
XLA Modules:
  0.0 83.4 jit_solution(15211299324418803858)
XLA Ops:
  0.6 2.4 %fusion.37 = (f32[2,192,1]{2,1,0:T(8,128)}, f32[2,192,1]{2,1,0:T(8,128)S(1)}, f32[2,192,1]{2,1,0:T(8,128)S(1)}, f32[2,192,1]{2,1,0:T(8,128)S(1)}, f32[2,192,1]{2,1,0:T(8,128)S(1)}, /*index=5*/f32[2,192,1]{2,1,0:T(8,128)S(1)}) fusion(f32[2,192,128]{2,1,0:T(8,128)} %param.14), kind=kLoop, calls=%fused_computation.78 | loop fusion | bytes 18432 | tf_op jit(solution)/shard_map/slice | solution.py:196
  3.1 0.1 copy.155
  3.2 0.1 copy.156
  3.3 0.1 copy.161
  3.4 0.1 copy.162
  4.1 0.1 copy.173
  4.3 0.1 copy.174
  4.6 0.1 copy.159
  4.7 0.1 copy.160
  4.8 0.7 copy.123
  5.5 0.1 fusion.34
  5.7 0.6 pad.15.surface
  6.3 0.6 pad.14.speeds
  7.0 0.7 pad_maximum_fusion.edges
  7.7 1.2 %fusion.5.windows = bf16[4,288,512]{2,1,0:T(8,128)(2,1)} fusion(bf16[288,3,64]{2,0,1:T(8,128)(2,1)S(1)} %get-tuple-element.25, bf16[288,3,64]{2,0,1:T(8,128)(2,1)S(1)} %get-tuple-element.24, bf16[288,4,384]{2,0,1:T(8,128)(2,1)S(1)} %copy.123), kind=kLoop, calls=%fused_computation.8 | loop fusion | flops 7077888 | bytes 2285568 | tf_op jit(solution)/shard_map/transpose | solution.py:357
  8.9 26.5 %exchange.1 = (bf16[1152,512]{1,0:T(8,128)(2,1)}, bf16[1152,128]{1,0:T(8,128)(2,1)}, f32[4,8,384]{2,1,0:T(8,128)}, bf16[1152,128]{1,0:T(8,128)(2,1)}, f32[32,1,128]{2,1,0:T(1,128)}) custom-call(bf16[4,288,512]{2,1,0:T(8,128)(2,1)} %fusion.5.windows, bf16[288,128]{1,0:T(8,128)(2,1)} %table.1, f32[8,384]{1,0:T(8,128)} %pad.14.speeds, ...), custom_call_target="tpu_custom_call" | custom-call | tf_op jit(solution)/shard_map/exchange/pallas_call | solution.py:169
  35.4 2.3 %fusion.42 = (bf16[384,128]{0,1:T(8,128)(2,1)S(1)}, f32[384,128]{0,1:T(8,128)}) fusion(bf16[1152,128]{1,0:T(8,128)(2,1)} %get-tuple-element.11, bf16[1152,512]{1,0:T(8,128)(2,1)} %get-tuple-element.7.win_ref), kind=kOutput, calls=%fused_computation.83 | convolution fusion | flops 113295360 | bytes 1474560 | tf_op jit(solution)/shard_map/dot_general | solution.py:378
  37.8 0.1 copy.143
  38.0 0.1 add.92
  38.1 0.2 convolution_convert_fusion
  38.3 0.7 copy.144
  39.0 3.5 %all-to-all-start = ((bf16[64,6,128]{2,1,0:T(8,128)(2,1)}), bf16[64,6,128]{2,1,0:T(8,128)(2,1)}, u32[]{:S(2)}, u32[]{:S(2)}) async-start(bf16[64,6,128]{2,1,0:T(8,128)(2,1)} %copy.144), calls=%async_computation | async-start | bytes 262144 | tf_op jit(solution)/shard_map/all_to_all | solution.py:414
  42.5 0.1 copy.157
  42.6 0.1 copy.158
  42.7 0.2 fusion.36
  43.3 0.3 select_reduce_fusion
  43.6 0.1 copy.168
  43.8 0.1 copy.172
  43.9 0.1 copy.166
  44.0 0.1 copy.167
  44.2 0.8 copy.170
  45.0 0.8 copy.171
  45.7 0.7 slice_bitcast_fusion.2
  46.6 0.3 fusion.43
  47.2 0.8 slice_bitcast_fusion
  48.0 0.2 copy.136
  48.3 0.7 dynamic-slice_convert_fusion
  49.2 29.7 %wave_step.1 = bf16[1152,384]{1,0:T(8,128)(2,1)S(1)} custom-call(bf16[1152,512]{1,0:T(8,128)(2,1)S(1)} %copy-done, bf16[1152,128]{1,0:T(8,128)(2,1)S(1)} %slice_select_fusion.near_ref, f32[1152,2]{1,0:T(8,128)S(1)} %bitcast.82, f32[2,512]{1,0:T(2,128)S(1)} %fusion.21.cur_ref, f32[1,384]{1,0:T(1,128)S(1)} %reshape.213.wet_ref, s32[3,4608]{1,0:T(4,128)S(1)} %copy-done.1, ...), custom_call_target="tpu_custom_call" | custom-call | flops 12230590464 | bytes 2359296 | tf_op jit(solution)/shard_map/wave_step/pallas_call | solution.py:282
  78.9 0.1 fusion.38
  79.1 0.1 copy.163
  79.2 0.1 copy.164
  79.3 1.5 %copy.140 = bf16[1152,384]{0,1:T(8,128)(2,1)} copy(bf16[1152,384]{1,0:T(8,128)(2,1)S(1)} %wave_step.1) | data formatting | bytes 1769472 | tf_op jit(solution)/shard_map/wave_step/pallas_call | solution.py:282
  80.8 1.0 %copy.145 = f32[32,2,6,128]{3,1,2,0:T(2,128)S(1)} copy(bf16[32,2,6,128]{3,2,1,0:T(8,128)(2,1)} %bitcast.30) | data formatting | bytes 294912 | tf_op jit(solution)/shard_map/convert_element_type | solution.py:416
  81.8 0.3 fusion.35
  82.1 0.1 copy.165
  82.2 0.1 copy.169
  82.4 0.1 fusion.12
  82.5 0.8 copy.154
  (64 shorter events, 1.9 us)
Async XLA Ops:
  0.6 2.9 %copy-start.11 = (s32[2,192]{1,0:T(2,128)S(1)}, s32[2,192]{1,0:T(2,128)}, u32[]{:S(2)}) copy-start(s32[2,192]{1,0:T(2,128)} %param.17) | copy-start | bytes 4612
  3.1 1.5 %copy-start.3 = (bf16[288,24,64]{0,2,1:T(8,128)(2,1)S(1)}, bf16[288,24,64]{0,2,1:T(8,128)(2,1)}, u32[]{:S(2)}) copy-start(bf16[288,24,64]{0,2,1:T(8,128)(2,1)} %param.9) | copy-start | bytes 2654212
  4.8 1.5 %copy-start.12 = (f32[2,288]{1,0:T(2,128)S(1)}, f32[2,288]{1,0:T(2,128)}, u32[]{:S(2)}) copy-start(f32[2,288]{1,0:T(2,128)} %param.10) | copy-start | bytes 6916
  35.4 2.5 %copy-start.13 = (s32[32]{0:T(128)S(1)}, s32[32]{0:T(128)}, u32[]{:S(2)}) copy-start(s32[32]{0:T(128)} %param.15) | copy-start | bytes 388
  35.4 7.3 %copy-start.2 = (f32[2,192,128]{2,1,0:T(8,128)S(1)}, f32[2,192,128]{2,1,0:T(8,128)}, u32[]{:S(2)}) copy-start(f32[2,192,128]{2,1,0:T(8,128)} %param.14) | copy-start | bytes 589828
  39.0 4.0 %copy-start.10 = (f32[32,1,128]{2,1,0:T(1,128)S(1)}, f32[32,1,128]{2,1,0:T(1,128)}, u32[]{:S(2)}) copy-start(f32[32,1,128]{2,1,0:T(1,128)} %get-tuple-element.10) | copy-start | bytes 49156
  39.0 41.8 %all-to-all-start = ((bf16[64,6,128]{2,1,0:T(8,128)(2,1)}), bf16[64,6,128]{2,1,0:T(8,128)(2,1)}, u32[]{:S(2)}, u32[]{:S(2)}) async-start(bf16[64,6,128]{2,1,0:T(8,128)(2,1)} %copy.144), calls=%async_computation | async-start | bytes 262144 | tf_op jit(solution)/shard_map/all_to_all | solution.py:414
  42.6 1.0 %copy-start.4 = (f32[2,192,1]{2,1,0:T(8,128)S(1)}, f32[2,192,1]{2,1,0:T(8,128)}, u32[]{:S(2)}) copy-start(f32[2,192,1]{2,1,0:T(8,128)} %get-tuple-element.34) | copy-start | bytes 4612
  43.0 3.5 %copy-start = (bf16[1152,512]{1,0:T(8,128)(2,1)S(1)}, bf16[1152,512]{1,0:T(8,128)(2,1)}, u32[]{:S(2)}) copy-start(bf16[1152,512]{1,0:T(8,128)(2,1)} %get-tuple-element.7.win_ref) | copy-start | bytes 3538948
  43.0 3.5 %copy-start.7 = (bf16[1152,128]{1,0:T(8,128)(2,1)S(1)}, bf16[1152,128]{1,0:T(8,128)(2,1)}, u32[]{:S(2)}) copy-start(bf16[1152,128]{1,0:T(8,128)(2,1)} %get-tuple-element.8) | copy-start | bytes 884740
  43.8 2.8 %copy-start.8 = (bf16[1152,128]{1,0:T(8,128)(2,1)S(1)}, bf16[1152,128]{1,0:T(8,128)(2,1)}, u32[]{:S(2)}) copy-start(bf16[1152,128]{1,0:T(8,128)(2,1)} %get-tuple-element.11) | copy-start | bytes 884740
  45.7 3.3 %copy-start.9 = (f32[4608]{0:T(1024)S(1)}, f32[4608]{0:T(1024)}, u32[]{:S(2)}) copy-start(f32[4608]{0:T(1024)} %param.13) | copy-start | bytes 55300
  46.5 2.7 %copy-start.1 = (s32[3,4608]{1,0:T(4,128)S(1)}, s32[3,4608]{1,0:T(4,128)}, u32[]{:S(2)}) copy-start(s32[3,4608]{1,0:T(4,128)} %ids_ref.1) | copy-start | bytes 165892
  80.8 1.6 %copy-start.5 = (f32[2,192,63]{1,2,0:T(8,128)S(1)}, f32[2,192,63]{1,2,0:T(8,128)}, u32[]{:S(2)}) copy-start(f32[2,192,63]{1,2,0:T(8,128)} %copy.170) | copy-start | bytes 290308
  80.8 1.6 %copy-start.6 = (f32[2,192,63]{1,2,0:T(8,128)S(1)}, f32[2,192,63]{1,2,0:T(8,128)}, u32[]{:S(2)}) copy-start(f32[2,192,63]{1,2,0:T(8,128)} %copy.171) | copy-start | bytes 290308

commit v3 on v2

--- a/solution.py
+++ b/solution.py
@@ -211,47 +211,90 @@
     return wet[..., None].astype(jnp.float32) * jnp.concatenate([new_east, new_north], axis=-1)
 
 
-def advect_block(ext, speed_x, speed_y, cur, wet, columns):
-    width = ext.shape[1] - 2 * columns
-    energy = ext
-    cx = speed_x + cur[0:1, :]
-    plus_x = jnp.maximum(cx, 0.0) * energy
-    minus_x = jnp.minimum(cx, 0.0) * energy
-    mid = slice(columns, columns + width)
-    moved = energy[:, mid] - plus_x[:, mid] + plus_x[:, :width]
-    moved = moved - minus_x[:, 2 * columns :] + minus_x[:, mid]
-    cy = speed_y + cur[1:2, :]
-    plus_y = jnp.maximum(cy, 0.0) * energy
-    minus_y = jnp.minimum(cy, 0.0) * energy
-    y = lax.rem(lax.broadcasted_iota(jnp.int32, (1, width), 1), columns)
-    plus_prev = jnp.where(y == 0, 0.0, plus_y[:, columns - 1 : columns - 1 + width])
-    minus_next = jnp.where(y == columns - 1, 0.0, minus_y[:, columns + 1 : columns + 1 + width])
-    moved = moved - plus_y[:, mid] + plus_prev - minus_next + minus_y[:, mid]
+def advect_block(energy, speeds, cur_x, cur_y, wet, columns):
+    cells = energy.shape[0] - 2 * columns
+    mid = slice(columns, columns + cells)
+    cx = speeds[0:1, :] + cur_x
+    from_before = jnp.maximum(cx[:cells], 0.0) * energy[:cells]
+    from_after = jnp.minimum(cx[2 * columns :], 0.0) * energy[2 * columns :]
+    own = energy[mid]
+    cy = speeds[1:2, :] + cur_y[mid]
+    plus = jnp.maximum(cy, 0.0) * own
+    minus = jnp.minimum(cy, 0.0) * own
+    y = lax.rem(lax.broadcasted_iota(jnp.int32, own.shape, 0), columns)
+    plus_prev = jnp.where(y == 0, 0.0, pltpu.roll(plus, 1, 0))
+    minus_next = jnp.where(y == columns - 1, 0.0, pltpu.roll(minus, cells - 1, 0))
+    moved = own - (jnp.abs(cx[mid]) + jnp.abs(cy)) * own
+    moved = moved + from_before - from_after + plus_prev - minus_next
     return (wet * moved).astype(jnp.bfloat16)
 
 
-def wave_kernel(columns, chunk, win_ref, near_ref, speeds_ref, cur_ref, wet_ref, ids_ref, coef_ref, out_ref, adv, adv_t, total):
+def wave_kernel(
+    columns,
+    chunk,
+    win_ref,
+    edges_ref,
+    mask_ref,
+    kernel_ref,
+    speeds_ref,
+    surface_ref,
+    wet_ref,
+    ids_ref,
+    coef_ref,
+    out_ref,
+    ext,
+    cur,
+    wet,
+    adv,
+    total,
+):
     step = pl.program_id(0)
-    bins = adv.shape[0]
+    cells, bins = adv.shape
+    levels = kernel_ref.shape[1] // 2
 
     @pl.when(step == 0)
     def _():
-        cur = cur_ref[...]
-        wet = wet_ref[...]
+        take_edge = mask_ref[...] > 0.0
+
+        def turn(i, carry):
+            rows = pl.ds(pl.multiple_of(i * chunk, chunk), chunk)
+            near = win_ref[rows, : 2 * columns].astype(jnp.float32)
+            near = jnp.where(take_edge, edges_ref[rows, :].astype(jnp.float32), near).T
+            main = win_ref[rows, 2 * columns :].astype(jnp.float32).T
+            ext[:columns, rows] = near[:columns].astype(jnp.bfloat16)
+            ext[columns : columns + cells, rows] = main.astype(jnp.bfloat16)
+            ext[columns + cells :, rows] = near[columns:].astype(jnp.bfloat16)
+            return carry
+
+        lax.fori_loop(0, bins // chunk, turn, 0)
+        drift = jnp.dot(ext[...], kernel_ref[...], preferred_element_type=jnp.float32)
+        half = DT_OCEAN * CORIOLIS
+
+        def wide(row):
+            return jnp.broadcast_to(row, (chunk, row.shape[1])).T
+
+        weight = half * wide(surface_ref[2:3, :])
+        cur[0] = CURRENT_SCALE * jnp.tanh(
+            wide(surface_ref[0:1, :]) + weight * drift[:, levels : levels + 1]
+        )
+        cur[1] = CURRENT_SCALE * jnp.tanh(
+            wide(surface_ref[1:2, :]) - weight * drift[:, 0:1]
+        )
+        wet[...] = wide(wet_ref[...])
 
         def one(i, carry):
-            rows = pl.ds(pl.multiple_of(i * chunk, chunk), chunk)
-            speeds = speeds_ref[rows, :]
-            near = near_ref[rows, :].astype(jnp.float32)
-            main = win_ref[rows, 2 * columns :].astype(jnp.float32)
-            ext = jnp.concatenate([near[:, :columns], main, near[:, columns:]], axis=1)
-            adv[rows, :] = advect_block(
-                ext, speeds[:, 0:1], speeds[:, 1:2], cur, wet, columns
+            lanes = pl.ds(pl.multiple_of(i * chunk, chunk), chunk)
+            adv[:, lanes] = advect_block(
+                ext[:, lanes].astype(jnp.float32),
+                speeds_ref[:, lanes],
+                cur[0],
+                cur[1],
+                wet[...],
+                columns,
             )
             return carry
 
         lax.fori_loop(0, bins // chunk, one, 0)
-        adv_t[...] = adv[...].T
         total[...] = jnp.zeros_like(total)
 
     block = ids_ref.shape[1]
@@ -260,11 +303,11 @@
     def onehot(which):
         return jnp.where(bin_ids == ids_ref[which : which + 1, :], 1.0, 0.0).astype(jnp.bfloat16)
 
-    first = jnp.dot(adv_t[...], onehot(0), preferred_element_type=jnp.float32)
-    second = jnp.dot(adv_t[...], onehot(1), preferred_element_type=jnp.float32)
+    first = jnp.dot(adv[...], onehot(0), preferred_element_type=jnp.float32)
+    second = jnp.dot(adv[...], onehot(1), preferred_element_type=jnp.float32)
     products = (coef_ref[...] * first * second).astype(jnp.bfloat16)
     total[...] += lax.dot_general(
-        onehot(2), products, (((1,), (1,)), ((), ())), preferred_element_type=jnp.float32
+        products, onehot(2), (((1,), (1,)), ((), ())), preferred_element_type=jnp.float32
     )
 
     @pl.when(step == pl.num_programs(0) - 1)
@@ -272,38 +315,42 @@
         out_ref[...] = (adv[...].astype(jnp.float32) + DT_SOURCE * total[...]).astype(jnp.bfloat16)
 
 
-def wave_step(win, near, speeds, cur, wet, pair_bins, pair_coef, columns):
+def wave_step(win, edges, mask, kernel_all, speeds, surface, wet, pair_bins, pair_coef, columns):
     bins, wide = win.shape
-    width = wide - 2 * columns
+    cells = wide - 2 * columns
     pairs = pair_bins.shape[1]
     block = 512 if pairs % 512 == 0 else pairs
+    chunk = 128 if bins % 128 == 0 else bins
     whole = lambda shape: pl.BlockSpec(shape, lambda i: (0, 0))
-    chunk = 32 if bins % 32 == 0 else bins
     return pl.pallas_call(
         functools.partial(wave_kernel, columns, chunk),
         grid=(pairs // block,),
-        out_shape=jax.ShapeDtypeStruct((bins, width), jnp.bfloat16),
+        out_shape=jax.ShapeDtypeStruct((cells, bins), jnp.bfloat16),
         in_specs=[
-            whole((bins, wide)),
-            whole((bins, 2 * columns)),
-            whole((bins, 2)),
-            whole((2, wide)),
-            whole((1, width)),
+            whole(win.shape),
+            whole(edges.shape),
+            whole(mask.shape),
+            whole(kernel_all.shape),
+            whole(speeds.shape),
+            whole(surface.shape),
+            whole(wet.shape),
             pl.BlockSpec((3, block), lambda i: (0, i)),
             pl.BlockSpec((1, block), lambda i: (0, i)),
         ],
-        out_specs=whole((bins, width)),
+        out_specs=whole((cells, bins)),
         scratch_shapes=[
-            pltpu.VMEM((bins, width), jnp.bfloat16),
-            pltpu.VMEM((width, bins), jnp.bfloat16),
-            pltpu.VMEM((bins, width), jnp.float32),
+            pltpu.VMEM((wide, bins), jnp.bfloat16),
+            pltpu.VMEM((2, wide, chunk), jnp.float32),
+            pltpu.VMEM((cells, chunk), jnp.float32),
+            pltpu.VMEM((cells, bins), jnp.bfloat16),
+            pltpu.VMEM((cells, bins), jnp.float32),
         ],
         compiler_params=pltpu.CompilerParams(vmem_limit_bytes=48 * 1024 * 1024),
         cost_estimate=pl.CostEstimate(
-            flops=6 * pairs * bins * width, bytes_accessed=4 * bins * wide, transcendentals=0
+            flops=6 * pairs * bins * cells, bytes_accessed=4 * bins * wide, transcendentals=0
         ),
         name="wave_step",
-    )(win, near, speeds, cur, wet, pair_bins, pair_coef[None, :])
+    )(win, edges, mask, kernel_all, speeds, surface, wet, pair_bins, pair_coef[None, :])
 
 
 def per_device(
@@ -366,39 +413,25 @@
     win, kernel_all, speeds, edges, surface = exchange(
         windows, stokes_kernel, speeds, edges, surface, space_count, bins_count
     )
-    speeds = jnp.transpose(speeds[:, :2, :local_bins], (0, 2, 1)).reshape(-1, 2)
+    speeds = jnp.transpose(speeds[:, :2, :local_bins], (1, 0, 2)).reshape(2, -1)
     space, part = lax.axis_index("space"), lax.axis_index("bins")
     from_below = (part == 0) & (space > 0)
     from_above = (part == bins_count - 1) & (space < space_count - 1)
     is_below = jnp.arange(2 * columns, dtype=jnp.int32) < columns
     take_edge = jnp.where(is_below, from_below, from_above)
-    near = jnp.where(take_edge[None, :], edges, win[:, : 2 * columns])
-
-    def project(cells):
-        return lax.dot_general(
-            cells, kernel_all, (((0,), (0,)), ((), ())), preferred_element_type=jnp.float32
-        )
-
-    drift_near, drift_main = project(near), project(win[:, 2 * columns :])
-
-    def in_order(cells_near, cells_main):
-        return jnp.concatenate([cells_near[:columns], cells_main, cells_near[columns:]])
-
+    take_edge = take_edge.astype(jnp.float32)[None, :]
+    drift_main = lax.dot_general(
+        win[:, 2 * columns :],
+        kernel_all,
+        (((0,), (0,)), ((), ())),
+        preferred_element_type=jnp.float32,
+    )
     mine = surface[:, 0, :used].reshape(groups, 3, group_cols, window_rows)
     mine = jnp.transpose(mine, (0, 2, 1, 3)).reshape(groups * group_cols, 3, window_rows)
     here = slot_col[:, None] == jnp.arange(columns, dtype=jnp.int32)[None, :]
     mine = jnp.sum(jnp.where(here[:, None, None, :], mine[:, :, :, None], 0.0), axis=0)
     mine = jnp.concatenate([mine[:, :1], mine[:, 2:], mine[:, 1:2]], axis=1)
     mine = mine.reshape(3, window_rows * columns)
-    half = DT_OCEAN * CORIOLIS
-    cur = CURRENT_SCALE * jnp.tanh(
-        jnp.stack(
-            [
-                mine[0] + half * mine[2] * in_order(drift_near[:, levels], drift_main[:, levels]),
-                mine[1] - half * mine[2] * in_order(drift_near[:, 0], drift_main[:, 0]),
-            ]
-        )
-    )
     wet_rows = lax.dynamic_slice_in_dim(
         wave_wet, lax.axis_index("bins") * block_rows, block_rows, 0
     )
@@ -416,8 +449,12 @@
     ).astype(jnp.float32)
     new_currents = ocean_step(currents, drift, ocean_wet, levels)
 
-    updated = wave_step(win, near, speeds, cur, wet_rows, pair_bins, pair_coef, columns)
-    new_spectrum = updated.reshape(bins_count * local_bins, block_rows, columns)
+    updated = wave_step(
+        win, edges, take_edge, kernel_all, speeds, mine, wet_rows, pair_bins, pair_coef, columns
+    )
+    new_spectrum = jnp.transpose(
+        updated.reshape(block_rows, columns, bins_count * local_bins), (2, 0, 1)
+    )
     return (new_spectrum, new_currents)
 
 

time: 84.2 us -> 69.1 us (0.82)
  Pallas kernels: 56.3 us -> 47 us
  local copies, waits for them, and re-layouts: 16.3 us -> 11.6 us
  matrix products: 2.86 us -> 1.94 us
    pallas_call x1, Pallas kernels: 29.7 us -> 20.4 us  [wave_step(): pl.pallas_call(functools.partial(wave_kernel, columns, chunk), grid=(pair...]
    pallas_call x1 -> x0, local copies, waits for them, and re-layouts: 1.49 us -> none  [wave_step(): pl.pallas_call(functools.partial(wave_kernel, columns, chunk), grid=(pair...]
    unnamed x51 -> x45, local copies, waits for them, and re-layouts: 4.62 us -> 3.31 us
    dot_general x2 -> x1, matrix products: 2.64 us -> 1.72 us  [per_device(): lax.dot_general(win[:, 2 * columns:], kernel_all, (((0,), (0,)), ((), ())...]
  transfers between devices with their start and end apart: 1 -> 1, of which waited for: 0 -> 0; matrix products, arithmetic and copies ran while one was open for 10% -> 6% of each run, Pallas kernels for 36% -> 30%
where the time goes in v3:
time: 69.1 us; the launch traced here: 68.3 us
  Pallas kernels  47 us (68%)
  local copies, waits for them, and re-layouts  11.6 us (17%)
  starting transfers between devices  3.46 us (5%)
  other arithmetic  3.31 us (5%)
  matrix products  1.94 us (3%)
  between operations  1.02 us (1%)
    pallas_call x1, Pallas kernels, exchange(): pl.pallas_call(functools.partial(exchange_kernel, space_count, bins_count...  26.5 us
    pallas_call x1, Pallas kernels, wave_step(): pl.pallas_call(functools.partial(wave_kernel, columns, chunk), grid=(pair...  20.4 us
    all_to_all x1, starting transfers between devices, per_device(): lax.all_to_all(routed, ('space', 'bins'), split_axis=0, concat_axis=1, ti...  3.46 us
    unnamed x45, local copies, waits for them, and re-layouts  3.31 us
    slice x2, local copies, waits for them, and re-layouts, levels_laplacian(): lower = jnp.concatenate([field[..., 1:], field[..., -1:]], axis=-1)  2.02 us
    dot_general x1, matrix products, per_device(): lax.dot_general(win[:, 2 * columns:], kernel_all, (((0,), (0,)), ((), ())...  1.72 us
  transfers between devices with their start and end apart: 1, of which 0 were waited for; matrix products, arithmetic and copies ran while one was open for 6% of the time, Pallas kernels for 30%

profile of v3, /device:TPU:1, one launch (start us, length us, event | category | flops | bytes accessed | tf_op | source)
XLA Modules:
  0.0 68.3 jit_solution(8845793591633154397)
XLA Ops:
  0.6 1.8 %fusion.33 = (f32[2,192,1]{2,1,0:T(8,128)S(1)}, f32[2,192,1]{2,1,0:T(8,128)S(1)}, f32[2,192,1]{2,1,0:T(8,128)S(1)}, f32[2,192,1]{2,1,0:T(8,128)S(1)}, f32[2,192,1]{2,1,0:T(8,128)S(1)}, /*index=5*/f32[2,192,1]{2,1,0:T(8,128)S(1)}) fusion(f32[2,192,128]{2,1,0:T(8,128)} %param.14), kind=kLoop, calls=%fused_computation.64 | loop fusion | bytes 18432 | tf_op jit(solution)/shard_map/slice | solution.py:196
  2.4 0.1 copy.145
  2.6 0.1 copy.146
  2.7 0.1 copy.151
  2.8 0.1 copy.152
  2.9 0.1 stack.24
  3.1 0.1 stack.25
  3.2 0.1 stack.26
  3.4 0.1 copy.126
  3.5 0.1 copy.163
  3.6 0.1 copy.164
  3.9 0.1 copy.149
  4.1 0.1 copy.150
  4.2 0.7 %copy.115 = bf16[288,4,384]{2,0,1:T(8,128)(2,1)S(1)} copy(bf16[288,4,384]{0,2,1:T(8,128)(2,1)S(1)} %bitcast.70) | data formatting | bytes 1769472 | tf_op jit(solution)/shard_map/reshape | solution.py:400
  4.9 0.1 fusion.30
  5.0 0.6 pad.15.surface
  5.7 0.6 pad.14.speeds
  6.3 0.1 add.82
  6.6 0.7 pad_maximum_fusion.edges
  7.2 1.2 %fusion.5.windows = bf16[4,288,512]{2,1,0:T(8,128)(2,1)} fusion(bf16[288,3,64]{2,0,1:T(8,128)(2,1)S(1)} %get-tuple-element.23, bf16[288,3,64]{2,0,1:T(8,128)(2,1)S(1)} %get-tuple-element.22, bf16[288,4,384]{2,0,1:T(8,128)(2,1)S(1)} %copy.115), kind=kLoop, calls=%fused_computation.8 | loop fusion | flops 7077888 | bytes 2285568 | tf_op jit(solution)/shard_map/transpose | solution.py:404
  8.5 26.5 %exchange.1 = (bf16[1152,512]{1,0:T(8,128)(2,1)}, bf16[1152,128]{1,0:T(8,128)(2,1)}, f32[4,8,384]{2,1,0:T(8,128)}, bf16[1152,128]{1,0:T(8,128)(2,1)}, f32[32,1,128]{2,1,0:T(1,128)}) custom-call(bf16[4,288,512]{2,1,0:T(8,128)(2,1)} %fusion.5.windows, bf16[288,128]{1,0:T(8,128)(2,1)} %table.1, f32[8,384]{1,0:T(8,128)} %pad.14.speeds, ...), custom_call_target="tpu_custom_call" | custom-call | tf_op jit(solution)/shard_map/exchange/pallas_call | solution.py:169
  35.0 1.7 %convolution_convert_fusion = bf16[384,128]{1,0:T(8,128)(2,1)S(1)} fusion(bf16[1152,128]{1,0:T(8,128)(2,1)} %get-tuple-element.9.kernel_ref, bf16[1152,512]{1,0:T(8,128)(2,1)} %get-tuple-element.7.win_ref), kind=kOutput, calls=%fused_computation.9 | convolution fusion | flops 113295360 | bytes 1277952 | tf_op jit(solution)/shard_map/dot_general | solution.py:423
  36.7 0.2 convolution_convert_fusion.1
  37.0 0.7 %copy.134 = bf16[64,6,128]{2,1,0:T(8,128)(2,1)} copy(bf16[64,6,128]{2,0,1:T(8,128)(2,1)S(1)} %convolution_convert_fusion.1) | data formatting | bytes 196608 | tf_op jit(solution)/shard_map/convert_element_type | solution.py:446
  37.7 3.5 %all-to-all-start = ((bf16[64,6,128]{2,1,0:T(8,128)(2,1)}), bf16[64,6,128]{2,1,0:T(8,128)(2,1)}, u32[]{:S(2)}, u32[]{:S(2)}) async-start(bf16[64,6,128]{2,1,0:T(8,128)(2,1)} %copy.134), calls=%async_computation | async-start | bytes 262144 | tf_op jit(solution)/shard_map/all_to_all | solution.py:447
  41.2 0.1 copy.147
  41.3 0.1 copy.148
  41.4 0.2 fusion.32
  41.8 0.1 copy.130
  42.0 0.3 select_reduce_fusion
  42.3 0.1 copy.158
  42.4 0.1 copy.162
  42.6 0.1 copy.156
  42.7 0.1 copy.157
  42.8 0.1 copy.160
  43.0 0.1 copy.161
  43.2 0.8 %slice_bitcast_fusion = f32[2,4,288]{2,0,1:T(2,128)S(1)} fusion(f32[4,8,384]{2,1,0:T(8,128)} %get-tuple-element.10), kind=kLoop, calls=%fused_computation.39 | loop fusion | bytes 18432 | tf_op jit(solution)/shard_map/transpose | solution.py:416
  44.1 0.7 %dynamic-slice_convert_fusion = f32[6,64]{1,0:T(8,128)S(1)} fusion(s32[24,64]{1,0:T(8,128)} %param.16, s32[]{:T(128)S(6)} %select_n.20), kind=kLoop, calls=%fused_computation.43 | loop fusion | flops 384 | bytes 3076 | tf_op jit(solution)/shard_map/convert_element_type | solution.py:438
  45.0 20.4 %wave_step.1 = bf16[384,1152]{1,0:T(8,128)(2,1)} custom-call(bf16[1152,512]{1,0:T(8,128)(2,1)S(1)} %copy-done, bf16[1152,128]{1,0:T(8,128)(2,1)S(1)} %copy-done.2, f32[1,128]{1,0:T(1,128)S(1)} %select_convert_fusion.mask_ref, bf16[1152,128]{1,0:T(8,128)(2,1)S(1)} %copy-done.1, f32[2,1152]{1,0:T(2,128)S(1)} %reshape.86.speeds_ref, ...), custom_call_target="tpu_custom_call" | custom-call | flops 12230590464 | bytes 2359296 | tf_op jit(solution)/shard_map/wave_step/pallas_call | solution.py:325
  65.4 0.1 fusion.34
  65.5 0.1 copy.153
  65.7 0.1 copy.154
  65.8 1.0 %copy.135 = f32[32,2,6,128]{3,1,2,0:T(2,128)S(1)} copy(bf16[32,2,6,128]{3,2,1,0:T(8,128)(2,1)} %bitcast.25) | data formatting | bytes 294912 | tf_op jit(solution)/shard_map/convert_element_type | solution.py:449
  66.8 0.3 fusion.31
  67.1 0.1 copy.155
  67.2 0.1 copy.159
  67.3 0.1 fusion.11
  67.5 0.8 %copy.144 = f32[2,192,128]{2,1,0:T(8,128)} copy(f32[2,192,128]{1,2,0:T(8,128)S(1)} %maximum_multiply_fusion) | data formatting | bytes 393216
  (48 shorter events, 1.1 us)
Async XLA Ops:
  0.6 2.3 %copy-start.8 = (s32[2,192]{1,0:T(2,128)S(1)}, s32[2,192]{1,0:T(2,128)}, u32[]{:S(2)}) copy-start(s32[2,192]{1,0:T(2,128)} %param.17) | copy-start | bytes 4612
  2.4 1.5 %copy-start.5 = (bf16[288,24,64]{0,2,1:T(8,128)(2,1)S(1)}, bf16[288,24,64]{0,2,1:T(8,128)(2,1)}, u32[]{:S(2)}) copy-start(bf16[288,24,64]{0,2,1:T(8,128)(2,1)} %param.9) | copy-start | bytes 2654212
  4.2 1.5 %copy-start.9 = (f32[2,288]{1,0:T(2,128)S(1)}, f32[2,288]{1,0:T(2,128)}, u32[]{:S(2)}) copy-start(f32[2,288]{1,0:T(2,128)} %param.10) | copy-start | bytes 6916
  4.2 2.1 %copy-start.10 = (s32[32]{0:T(128)S(1)}, s32[32]{0:T(128)}, u32[]{:S(2)}) copy-start(s32[32]{0:T(128)} %param.15) | copy-start | bytes 388
  35.0 6.4 %copy-start.4 = (f32[2,192,128]{2,1,0:T(8,128)S(1)}, f32[2,192,128]{2,1,0:T(8,128)}, u32[]{:S(2)}) copy-start(f32[2,192,128]{2,1,0:T(8,128)} %param.14) | copy-start | bytes 589828
  37.7 4.0 %copy-start.7 = (f32[32,1,128]{2,1,0:T(1,128)S(1)}, f32[32,1,128]{2,1,0:T(1,128)}, u32[]{:S(2)}) copy-start(f32[32,1,128]{2,1,0:T(1,128)} %get-tuple-element.11) | copy-start | bytes 49156
  37.7 28.1 %all-to-all-start = ((bf16[64,6,128]{2,1,0:T(8,128)(2,1)}), bf16[64,6,128]{2,1,0:T(8,128)(2,1)}, u32[]{:S(2)}, u32[]{:S(2)}) async-start(bf16[64,6,128]{2,1,0:T(8,128)(2,1)} %copy.134), calls=%async_computation | async-start | bytes 262144 | tf_op jit(solution)/shard_map/all_to_all | solution.py:447
  41.9 3.0 %copy-start.6 = (f32[4608]{0:T(1024)S(1)}, f32[4608]{0:T(1024)}, u32[]{:S(2)}) copy-start(f32[4608]{0:T(1024)} %param.13) | copy-start | bytes 55300
  41.9 3.0 %copy-start = (bf16[1152,512]{1,0:T(8,128)(2,1)S(1)}, bf16[1152,512]{1,0:T(8,128)(2,1)}, u32[]{:S(2)}) copy-start(bf16[1152,512]{1,0:T(8,128)(2,1)} %get-tuple-element.7.win_ref) | copy-start | bytes 3538948
  41.9 3.0 %copy-start.1 = (bf16[1152,128]{1,0:T(8,128)(2,1)S(1)}, bf16[1152,128]{1,0:T(8,128)(2,1)}, u32[]{:S(2)}) copy-start(bf16[1152,128]{1,0:T(8,128)(2,1)} %get-tuple-element.9.kernel_ref) | copy-start | bytes 884740
  41.9 3.0 %copy-start.2 = (bf16[1152,128]{1,0:T(8,128)(2,1)S(1)}, bf16[1152,128]{1,0:T(8,128)(2,1)}, u32[]{:S(2)}) copy-start(bf16[1152,128]{1,0:T(8,128)(2,1)} %get-tuple-element.8.edges_ref) | copy-start | bytes 884740
  41.9 3.0 %copy-start.3 = (s32[3,4608]{1,0:T(4,128)S(1)}, s32[3,4608]{1,0:T(4,128)}, u32[]{:S(2)}) copy-start(s32[3,4608]{1,0:T(4,128)} %ids_ref.1) | copy-start | bytes 165892

commit v4 on v3

--- a/solution.py
+++ b/solution.py
@@ -161,7 +161,7 @@
 
 
 def exchange(windows, table, speeds, edges, surface, space_count, bins_count):
-    anywhere = pl.BlockSpec(memory_space=pl.ANY)
+    here = pl.BlockSpec(memory_space=pltpu.VMEM)
     local_bins = table.shape[0]
     bins = local_bins * bins_count
     total = space_count * bins_count
@@ -175,8 +175,8 @@
             jax.ShapeDtypeStruct((bins, edges.shape[2]), edges.dtype),
             jax.ShapeDtypeStruct(surface.shape, surface.dtype),
         ),
-        in_specs=[anywhere] * 5,
-        out_specs=(anywhere,) * 5,
+        in_specs=[here] * 5,
+        out_specs=(here,) * 5,
         scratch_shapes=[
             dma((4,)),
             dma((3, bins_count)),
@@ -186,29 +186,41 @@
             dma((total,)),
             dma((total,)),
         ],
-        compiler_params=pltpu.CompilerParams(collective_id=0, has_side_effects=True),
+        compiler_params=pltpu.CompilerParams(
+            collective_id=0, has_side_effects=True, vmem_limit_bytes=32 * 1024 * 1024
+        ),
         name="exchange",
     )(windows, table, speeds, edges, surface)
 
 
-def levels_laplacian(field):
-    upper = jnp.concatenate([field[..., :1], field[..., :-1]], axis=-1)
-    lower = jnp.concatenate([field[..., 1:], field[..., -1:]], axis=-1)
-    return upper + lower - 2.0 * field
+def ocean_kernel(levels, currents_ref, drift_ref, wet_ref, out_ref, drift):
+    slots, rows, lanes = currents_ref.shape
+    sources, block_rows = drift_ref.shape[0] // slots, drift_ref.shape[1]
+    lane = lax.broadcasted_iota(jnp.int32, (rows, lanes), 1)
+    level = lax.rem(lane, levels)
+    turn = jnp.where(lane < levels, CORIOLIS, -CORIOLIS)
+    for slot in range(slots):
+        for source in range(sources):
+            drift[source * block_rows : (source + 1) * block_rows, :] = drift_ref[
+                source * slots + slot
+            ].astype(jnp.float32)
+        field = currents_ref[slot]
+        upper = jnp.where(level == 0, field, pltpu.roll(field, 1, 1))
+        lower = jnp.where(level == levels - 1, field, pltpu.roll(field, lanes - 1, 1))
+        other = pltpu.roll(field + drift[...], levels, 1)
+        moved = field + DT_OCEAN * (turn * other + MIXING * (upper + lower - 2.0 * field))
+        wet = jnp.broadcast_to(wet_ref[slot : slot + 1, :].astype(jnp.float32), (lanes, rows)).T
+        out_ref[slot] = wet * moved
 
 
 def ocean_step(currents, drift, wet, levels):
-    east = currents[..., :levels]
-    north = currents[..., levels:]
-    east_drift = drift[..., :levels]
-    north_drift = drift[..., levels:]
-    new_east = east + DT_OCEAN * (
-        CORIOLIS * (north + north_drift) + MIXING * levels_laplacian(east)
-    )
-    new_north = north + DT_OCEAN * (
-        -CORIOLIS * (east + east_drift) + MIXING * levels_laplacian(north)
-    )
-    return wet[..., None].astype(jnp.float32) * jnp.concatenate([new_east, new_north], axis=-1)
+    return pl.pallas_call(
+        functools.partial(ocean_kernel, levels),
+        out_shape=jax.ShapeDtypeStruct(currents.shape, currents.dtype),
+        scratch_shapes=[pltpu.VMEM(currents.shape[1:], jnp.float32)],
+        compiler_params=pltpu.CompilerParams(vmem_limit_bytes=16 * 1024 * 1024),
+        name="ocean_step",
+    )(currents, drift, wet)
 
 
 def advect_block(energy, speeds, cur_x, cur_y, wet, columns):
@@ -445,8 +457,8 @@
         preferred_element_type=jnp.float32,
     ).astype(jnp.bfloat16)
     drift = lax.all_to_all(
-        routed, ("space", "bins"), split_axis=0, concat_axis=1, tiled=True
-    ).astype(jnp.float32)
+        routed, ("space", "bins"), split_axis=0, concat_axis=0, tiled=True
+    )
     new_currents = ocean_step(currents, drift, ocean_wet, levels)
 
     updated = wave_step(

time: 69.1 us -> 61.3 us (0.89)
  local copies, waits for them, and re-layouts: 11.6 us -> 6.28 us
  other arithmetic: 3.31 us -> 1.48 us
  matrix products: 1.94 us -> 0.67 us
  Pallas kernels: 47 us -> 47.8 us
    unnamed x45 -> x26, local copies, waits for them, and re-layouts: 3.31 us -> 1.67 us
    dot_general x1, matrix products: 1.72 us -> 0.45 us  [per_device(): lax.dot_general(win[:, 2 * columns:], kernel_all, (((0,), (0,)), ((), ())...]
    transpose x1, other arithmetic: 1.23 us -> 0.2 us  [per_device(): jnp.transpose(jnp.concatenate([before, after, rows], axis=2), (1, 0, 2))]
    pallas_call x0 -> x1, Pallas kernels: none -> 0.99 us  [ocean_step(): pl.pallas_call(functools.partial(ocean_kernel, levels), out_shape=jax.Sha...]
    convert_element_type x1 -> x0, local copies, waits for them, and re-layouts: 0.98 us -> none  [per_device(): drift = lax.all_to_all(routed, ('space', 'bins'), split_axis=0, concat_ax...]
    transpose x2, local copies, waits for them, and re-layouts: 0.81 us -> 0.01 us  [per_device(): speeds = jnp.transpose(speeds[:, :2, :local_bins], (1, 0, 2)).reshape(2, -1)]
    slice x4 -> x1, local copies, waits for them, and re-layouts: 2.4 us -> 1.72 us  [per_device(): v0, v1 = (currents[:, :, levels], currents[:, :, levels + 1])]
  transfers between devices with their start and end apart: 1 -> 1, of which waited for: 0 -> 0; matrix products, arithmetic and copies ran while one was open for 6% -> 3% of each run, Pallas kernels for 30% -> 34%
where the time goes in v4:
time: 61.3 us; the launch traced here: 60.8 us
  Pallas kernels  47.8 us (78%)
  local copies, waits for them, and re-layouts  6.28 us (10%)
  starting transfers between devices  3.68 us (6%)
  other arithmetic  1.48 us (2%)
  between operations  0.96 us (2%)
  matrix products  0.67 us (1%)
    pallas_call x1, Pallas kernels, exchange(): pl.pallas_call(functools.partial(exchange_kernel, space_count, bins_count...  26.3 us
    pallas_call x1, Pallas kernels, wave_step(): pl.pallas_call(functools.partial(wave_kernel, columns, chunk), grid=(pair...  20.5 us
    all_to_all x1, starting transfers between devices, per_device(): lax.all_to_all(routed, ('space', 'bins'), split_axis=0, concat_axis=0, ti...  3.68 us
    slice x1, local copies, waits for them, and re-layouts, per_device(): v0, v1 = (currents[:, :, levels], currents[:, :, levels + 1])  1.72 us
    unnamed x26, local copies, waits for them, and re-layouts  1.67 us
  transfers between devices with their start and end apart: 1, of which 0 were waited for; matrix products, arithmetic and copies ran while one was open for 3% of the time, Pallas kernels for 34%

profile of v4, /device:TPU:1, one launch (start us, length us, event | category | flops | bytes accessed | tf_op | source)
XLA Modules:
  0.0 60.8 jit_solution(2805000923679189292)
XLA Ops:
  0.6 1.7 %fusion.22 = (f32[2,192,1]{2,1,0:T(8,128)S(1)}, f32[2,192,1]{2,1,0:T(8,128)S(1)}, f32[2,192,1]{2,1,0:T(8,128)S(1)}, f32[2,192,1]{2,1,0:T(8,128)S(1)}) fusion(f32[2,192,128]{2,1,0:T(8,128)} %currents_ref.1), kind=kLoop, calls=%fused_computation.49 | loop fusion | bytes 12288 | tf_op jit(solution)/shard_map/slice | solution.py:393
  2.4 0.0 copy-start.4
  2.4 0.1 copy.100
  2.5 0.1 copy.97
  2.6 0.1 copy.98
  2.7 0.1 copy.99
  2.9 0.1 stack.24
  3.0 0.1 stack.25
  3.1 0.1 stack.26
  3.2 0.1 fusion.23
  3.3 0.1 copy.88
  3.4 0.1 copy.101
  3.5 0.1 copy.102
  3.7 0.1 fusion.8
  3.8 0.1 copy.89
  3.9 0.1 copy.95
  4.0 0.1 copy.96
  4.1 0.0 copy-start.6
  4.1 0.0 copy-start.7
  4.1 0.7 %copy.77 = bf16[288,4,384]{2,0,1:T(8,128)(2,1)S(1)} copy(bf16[288,4,384]{0,2,1:T(8,128)(2,1)S(1)} %bitcast.63) | data formatting | bytes 1769472 | tf_op jit(solution)/shard_map/reshape | solution.py:412
  4.8 0.1 fusion.21
  5.0 0.0 copy-done.6
  5.0 0.1 iota_add_fusion
  5.1 0.1 add.58
  5.2 0.1 pad_bitcast_fusion
  5.3 0.0 copy-start.1
  5.3 0.2 fusion.5.windows
  5.6 0.7 %copy-done.1 = bf16[288,128]{1,0:T(8,128)(2,1)S(1)} copy-done((bf16[288,128]{1,0:T(8,128)(2,1)S(1)}, bf16[288,128]{1,0:T(8,128)(2,1)}, u32[]{:S(2)}) %copy-start.1) | copy-done | bytes 73752
  6.2 26.3 %exchange.1 = (bf16[1152,512]{1,0:T(8,128)(2,1)S(1)}, bf16[1152,128]{1,0:T(8,128)(2,1)S(1)}, f32[4,8,384]{2,1,0:T(8,128)S(1)}, bf16[1152,128]{1,0:T(8,128)(2,1)S(1)}, f32[32,1,128]{2,1,0:T(1,128)S(1)}) custom-call(bf16[4,288,512]{2,1,0:T(8,128)(2,1)S(1)} %fusion.5.windows, bf16[288,128]{1,0:T(8,128)(2,1)S(1)} %copy-done.1, f32[8,384]{1,0:T(8,128)S(1)} %pad.14.speeds, ...), custom_call_target="tpu_custom_call" | custom-call | tf_op jit(solution)/shard_map/exchange/pallas_call | solution.py:169
  32.6 0.0 copy-start.5
  32.6 0.0 copy-start.3
  32.6 0.5 convolution_convert_fusion
  33.0 0.2 convolution_convert_fusion.1
  33.3 0.7 %copy.94 = bf16[64,6,128]{2,1,0:T(8,128)(2,1)} copy(bf16[64,6,128]{2,0,1:T(8,128)(2,1)S(1)} %convolution_convert_fusion.1) | data formatting | bytes 196608 | tf_op jit(solution)/shard_map/convert_element_type | solution.py:458
  34.0 3.7 %all-to-all-start = ((bf16[64,6,128]{2,1,0:T(8,128)(2,1)}), bf16[64,6,128]{2,1,0:T(8,128)(2,1)S(1)}, u32[]{:S(2)}, u32[]{:S(2)}) async-start(bf16[64,6,128]{2,1,0:T(8,128)(2,1)} %copy.94), calls=%async_computation | async-start | bytes 262144 | tf_op jit(solution)/shard_map/all_to_all | solution.py:459
  37.7 0.1 iota_compare_fusion.5
  37.8 0.1 copy.91
  37.8 0.1 copy.92
  37.9 0.1 copy.93
  38.0 0.3 select_reduce_fusion
  38.3 0.1 reshape.81.surface_ref
  38.4 0.1 reshape.80.speeds_ref
  38.5 0.7 %dynamic-slice_convert_fusion = f32[6,64]{1,0:T(8,128)S(1)} fusion(s32[24,64]{1,0:T(8,128)} %param.16, s32[]{:T(128)S(6)} %select_n.20), kind=kLoop, calls=%fused_computation.30 | loop fusion | flops 384 | bytes 3076 | tf_op jit(solution)/shard_map/convert_element_type | solution.py:450
  39.2 0.1 reshape.82.wet_ref
  39.4 0.0 copy-start
  39.4 20.5 %wave_step.1 = bf16[384,1152]{1,0:T(8,128)(2,1)} custom-call(bf16[1152,512]{1,0:T(8,128)(2,1)S(1)} %get-tuple-element.7.win_ref, bf16[1152,128]{1,0:T(8,128)(2,1)S(1)} %get-tuple-element.8.edges_ref, f32[1,128]{1,0:T(1,128)S(1)} %select_convert_fusion.mask_ref, bf16[1152,128]{1,0:T(8,128)(2,1)S(1)} %get-tuple-element.9.kernel_ref, ...), custom_call_target="tpu_custom_call" | custom-call | flops 12230590464 | bytes 2359296 | tf_op jit(solution)/shard_map/wave_step/pallas_call | solution.py:337
  59.8 0.0 all-to-all-done.drift_ref
  59.8 1.0 %ocean_step.1 = f32[2,192,128]{2,1,0:T(8,128)} custom-call(f32[2,192,128]{2,1,0:T(8,128)S(1)} %copy-done, bf16[64,6,128]{2,1,0:T(8,128)(2,1)S(1)} %all-to-all-done.drift_ref, s32[2,192]{1,0:T(2,128)S(1)} %copy-done.2), custom_call_target="tpu_custom_call" | custom-call | tf_op jit(solution)/shard_map/ocean_step/pallas_call | solution.py:217
  (24 shorter events, 0.2 us)
Async XLA Ops:
  0.6 2.2 %copy-start.2 = (s32[2,192]{1,0:T(2,128)S(1)}, s32[2,192]{1,0:T(2,128)}, u32[]{:S(2)}) copy-start(s32[2,192]{1,0:T(2,128)} %wet_ref.1) | copy-start | bytes 4612
  2.4 1.5 %copy-start.4 = (bf16[288,24,64]{0,2,1:T(8,128)(2,1)S(1)}, bf16[288,24,64]{0,2,1:T(8,128)(2,1)}, u32[]{:S(2)}) copy-start(bf16[288,24,64]{0,2,1:T(8,128)(2,1)} %param.9) | copy-start | bytes 2654212
  4.1 0.9 %copy-start.6 = (f32[2,288]{1,0:T(2,128)S(1)}, f32[2,288]{1,0:T(2,128)}, u32[]{:S(2)}) copy-start(f32[2,288]{1,0:T(2,128)} %param.10) | copy-start | bytes 6916
  4.1 0.9 %copy-start.7 = (s32[32]{0:T(128)S(1)}, s32[32]{0:T(128)}, u32[]{:S(2)}) copy-start(s32[32]{0:T(128)} %param.15) | copy-start | bytes 388
  5.3 0.9 %copy-start.1 = (bf16[288,128]{1,0:T(8,128)(2,1)S(1)}, bf16[288,128]{1,0:T(8,128)(2,1)}, u32[]{:S(2)}) copy-start(bf16[288,128]{1,0:T(8,128)(2,1)} %table.1) | copy-start | bytes 221188
  32.6 6.8 %copy-start.5 = (f32[4608]{0:T(1024)S(1)}, f32[4608]{0:T(1024)}, u32[]{:S(2)}) copy-start(f32[4608]{0:T(1024)} %param.13) | copy-start | bytes 55300
  32.6 6.8 %copy-start.3 = (s32[3,4608]{1,0:T(4,128)S(1)}, s32[3,4608]{1,0:T(4,128)}, u32[]{:S(2)}) copy-start(s32[3,4608]{1,0:T(4,128)} %ids_ref.1) | copy-start | bytes 165892
  34.0 25.9 %all-to-all-start = ((bf16[64,6,128]{2,1,0:T(8,128)(2,1)}), bf16[64,6,128]{2,1,0:T(8,128)(2,1)S(1)}, u32[]{:S(2)}, u32[]{:S(2)}) async-start(bf16[64,6,128]{2,1,0:T(8,128)(2,1)} %copy.94), calls=%async_computation | async-start | bytes 262144 | tf_op jit(solution)/shard_map/all_to_all | solution.py:459
  39.4 20.5 %copy-start = (f32[2,192,128]{2,1,0:T(8,128)S(1)}, f32[2,192,128]{2,1,0:T(8,128)}, u32[]{:S(2)}) copy-start(f32[2,192,128]{2,1,0:T(8,128)} %currents_ref.1) | copy-start | bytes 589828

commit v5 on v4

--- a/solution.py
+++ b/solution.py
@@ -11,6 +11,40 @@
 MIXING = 0.4
 CURRENT_SCALE = 0.15
 DT_SOURCE = 0.5
+
+
+def surface_kernel(levels, block_rows, currents_ref, wet_ref, out_ref, held):
+    slots, rows, lanes = currents_ref.shape
+    groups = rows // block_rows
+    held[...] = jnp.zeros_like(held)
+    for slot in range(slots):
+        wet = jnp.broadcast_to(wet_ref[slot : slot + 1, :].astype(jnp.float32), (lanes, rows)).T
+        field = currents_ref[slot]
+        below = pltpu.roll(field, lanes - 1, 1)
+        other = pltpu.roll(field, levels, 1)
+        lane = lax.broadcasted_iota(jnp.int32, (rows, lanes), 1)
+        turn = jnp.where(lane < levels, CORIOLIS, -CORIOLIS)
+        moved = wet * (field + DT_OCEAN * (turn * other + MIXING * (below - field)))
+        inner = pl.ds(8, rows)
+        held[inner, slot : slot + 1] = moved[:, 0:1]
+        held[inner, slots + slot : slots + slot + 1] = moved[:, levels : levels + 1]
+        held[inner, 2 * slots + slot : 2 * slots + slot + 1] = wet[:, 0:1]
+    sent = jnp.zeros((groups, lanes), jnp.float32)
+    for row in range(block_rows + 2):
+        part = held[pl.ds(7 + row, groups, stride=block_rows), :]
+        sent = sent + (pltpu.roll(part, 8 * row, 1) if row else part)
+    out_ref[...] = sent
+
+
+def surface_windows(currents, wet, levels, block_rows):
+    rows, lanes = currents.shape[1:]
+    return pl.pallas_call(
+        functools.partial(surface_kernel, levels, block_rows),
+        out_shape=jax.ShapeDtypeStruct((rows // block_rows, lanes), jnp.float32),
+        scratch_shapes=[pltpu.VMEM((rows + 16, lanes), jnp.float32)],
+        compiler_params=pltpu.CompilerParams(vmem_limit_bytes=16 * 1024 * 1024),
+        name="surface_windows",
+    )(currents, wet)
 
 
 def exchange_kernel(
@@ -388,26 +422,8 @@
         col_map[:, None] * group_cols + jnp.arange(group_cols, dtype=jnp.int32)[None, :]
     ).reshape(-1)
 
-    wet_f = ocean_wet.astype(jnp.float32)
-    u0, u1 = currents[:, :, 0], currents[:, :, 1]
-    v0, v1 = currents[:, :, levels], currents[:, :, levels + 1]
-    su = wet_f * (u0 + DT_OCEAN * (CORIOLIS * v0 + MIXING * (u1 - u0)))
-    sv = wet_f * (v0 + DT_OCEAN * (-CORIOLIS * u0 + MIXING * (v1 - v0)))
-    surface = jnp.stack([su, sv, wet_f])
-
-    def windows_of(rows, before, after):
-        before = jnp.concatenate([before, rows[..., :-1, -1:]], axis=-2)
-        after = jnp.concatenate([rows[..., 1:, :1], after], axis=-2)
-        return jnp.concatenate([before, after, rows], axis=-1)
-
-    none = jnp.zeros((3, group_cols, 1, 1), jnp.float32)
-    surface = windows_of(
-        surface.reshape(3, group_cols, groups, block_rows), none, none
-    )
     window_rows = block_rows + 2
-    surface = jnp.transpose(surface, (2, 0, 1, 3)).reshape(groups, 1, 3 * group_cols * window_rows)
-    used = surface.shape[2]
-    surface = jnp.pad(surface, ((0, 0), (0, 0), (0, -used % 128)))
+    surface = surface_windows(currents, ocean_wet, levels, block_rows)[:, None, :]
 
     rows = spectrum.reshape(local_bins, bins_count, width)
     zeros = jnp.zeros((local_bins, 1, columns), spectrum.dtype)
@@ -438,16 +454,15 @@
         (((0,), (0,)), ((), ())),
         preferred_element_type=jnp.float32,
     )
-    mine = surface[:, 0, :used].reshape(groups, 3, group_cols, window_rows)
-    mine = jnp.transpose(mine, (0, 2, 1, 3)).reshape(groups * group_cols, 3, window_rows)
+    mine = surface[:, 0, : 8 * window_rows].reshape(groups, window_rows, 8)
+    mine = mine[:, :, : 3 * group_cols].reshape(groups, window_rows, 3, group_cols)
+    mine = jnp.transpose(mine, (0, 3, 2, 1)).reshape(groups * group_cols, 3, window_rows)
     here = slot_col[:, None] == jnp.arange(columns, dtype=jnp.int32)[None, :]
     mine = jnp.sum(jnp.where(here[:, None, None, :], mine[:, :, :, None], 0.0), axis=0)
-    mine = jnp.concatenate([mine[:, :1], mine[:, 2:], mine[:, 1:2]], axis=1)
     mine = mine.reshape(3, window_rows * columns)
-    wet_rows = lax.dynamic_slice_in_dim(
-        wave_wet, lax.axis_index("bins") * block_rows, block_rows, 0
-    )
-    wet_rows = wet_rows.astype(jnp.float32).reshape(1, width)
+    wet_rows = wave_wet.astype(jnp.float32).reshape(bins_count, block_rows, columns)
+    is_mine = jnp.arange(bins_count, dtype=jnp.int32) == part
+    wet_rows = jnp.sum(jnp.where(is_mine[:, None, None], wet_rows, 0.0), axis=0).reshape(1, width)
 
     inner = drift_main.reshape(block_rows, columns, 2 * levels)
     routed = jnp.einsum(

time: 61.3 us -> 59.9 us (0.977)
  local copies, waits for them, and re-layouts: 6.28 us -> 5.02 us
  other arithmetic: 1.48 us -> 0.73 us
    slice x5 -> x2, local copies, waits for them, and re-layouts: 1.89 us -> 0.09 us  [the longest x1 0.08 us: per_device(): mine = surface[:, 0, :8 * window_rows].reshape(groups, window_rows, 8)]
    reshape x1, local copies, waits for them, and re-layouts: 0.69 us -> 1.62 us  [per_device(): rows = spectrum.reshape(local_bins, bins_count, width)]
    slice x1, local copies, waits for them, and re-layouts: 0.02 us -> 0.84 us  [per_device(): spectrum[:, -1, :]]
    convert_element_type x2 -> x1, other arithmetic: 0.71 us -> 0.01 us  [per_device(): wave_wet.astype(jnp.float32).reshape(bins_count, block_rows, columns)]
    unnamed x26 -> x18, local copies, waits for them, and re-layouts: 1.67 us -> 0.97 us
  transfers between devices with their start and end apart: 1 -> 1, of which waited for: 0 -> 0; matrix products, arithmetic and copies ran while one was open for 3% -> 2% of each run, Pallas kernels for 34% -> 34%
where the time goes in v5:
time: 59.9 us; the launch traced here: 59.4 us
  Pallas kernels  48.4 us (81%)
  local copies, waits for them, and re-layouts  5.02 us (8%)
  starting transfers between devices  3.67 us (6%)
  between operations  0.92 us (2%)
  other arithmetic  0.73 us (1%)
  matrix products  0.67 us (1%)
    pallas_call x1, Pallas kernels, exchange(): pl.pallas_call(functools.partial(exchange_kernel, space_count, bins_count...  26.4 us
    pallas_call x1, Pallas kernels, wave_step(): pl.pallas_call(functools.partial(wave_kernel, columns, chunk), grid=(pair...  20.5 us
    all_to_all x1, starting transfers between devices, per_device(): lax.all_to_all(routed, ('space', 'bins'), split_axis=0, concat_axis=0, ti...  3.67 us
    reshape x1, local copies, waits for them, and re-layouts, per_device(): rows = spectrum.reshape(local_bins, bins_count, width)  1.62 us
  transfers between devices with their start and end apart: 1, of which 0 were waited for; matrix products, arithmetic and copies ran while one was open for 2% of the time, Pallas kernels for 34%

profile of v5, /device:TPU:1, one launch (start us, length us, event | category | flops | bytes accessed | tf_op | source)
XLA Modules:
  0.0 59.4 jit_solution(12028307819387681398)
XLA Ops:
  0.6 0.8 %fusion.8 = (bf16[288,1,64]{0,2,1:T(8,128)(2,1)S(1)}, bf16[288,1,64]{0,2,1:T(8,128)(2,1)S(1)}) fusion(bf16[288,24,64]{0,2,1:T(8,128)(2,1)} %param.9), kind=kLoop, calls=%fused_computation.24 | loop fusion | bytes 147456 | tf_op jit(solution)/shard_map/slice | solution.py:436
  1.5 0.1 copy.48
  1.6 0.1 copy.49
  1.7 0.0 copy-start.7
  1.7 1.6 %copy.37 = bf16[288,4,384]{2,0,1:T(8,128)(2,1)S(1)} copy(bf16[288,4,384]{0,2,1:T(8,128)(2,1)} %bitcast.30) | data formatting | bytes 1769472 | tf_op jit(solution)/shard_map/reshape | solution.py:428
  3.4 0.1 fusion.9
  3.5 0.0 copy-done.7
  3.5 0.1 iota_add_fusion
  3.6 0.1 add.33
  3.7 0.1 pad_bitcast_fusion
  3.8 0.0 copy-start
  3.8 0.0 copy-start.2
  3.8 0.0 copy-start.6
  3.8 0.0 copy-start.1
  3.9 0.2 fusion.5.windows
  4.1 0.7 %copy-done = f32[2,192,128]{2,1,0:T(8,128)S(1)} copy-done((f32[2,192,128]{2,1,0:T(8,128)S(1)}, f32[2,192,128]{2,1,0:T(8,128)}, u32[]{:S(2)}) %copy-start) | copy-done | bytes 196632
  4.7 0.0 copy-done.2
  4.7 0.6 surface_windows.1
  5.3 0.0 copy-done.6
  5.4 0.0 copy-done.1
  5.4 26.4 %exchange.1 = (bf16[1152,512]{1,0:T(8,128)(2,1)S(1)}, bf16[1152,128]{1,0:T(8,128)(2,1)S(1)}, f32[4,8,384]{2,1,0:T(8,128)S(1)}, bf16[1152,128]{1,0:T(8,128)(2,1)S(1)}, f32[32,1,128]{2,1,0:T(1,128)S(1)}) custom-call(bf16[4,288,512]{2,1,0:T(8,128)(2,1)S(1)} %fusion.5.windows, bf16[288,128]{1,0:T(8,128)(2,1)S(1)} %copy-done.1, f32[8,384]{1,0:T(8,128)S(1)} %pad.8.speeds, ...), custom_call_target="tpu_custom_call" | custom-call | tf_op jit(solution)/shard_map/exchange/pallas_call | solution.py:203
  31.7 0.0 copy-start.5
  31.8 0.0 copy-start.4
  31.8 0.0 copy-start.3
  31.8 0.5 convolution_convert_fusion
  32.2 0.2 convolution_convert_fusion.1
  32.5 0.7 %copy.47 = bf16[64,6,128]{2,1,0:T(8,128)(2,1)} copy(bf16[64,6,128]{2,0,1:T(8,128)(2,1)S(1)} %convolution_convert_fusion.1) | data formatting | bytes 196608 | tf_op jit(solution)/shard_map/convert_element_type | solution.py:473
  33.2 3.7 %all-to-all-start = ((bf16[64,6,128]{2,1,0:T(8,128)(2,1)}), bf16[64,6,128]{2,1,0:T(8,128)(2,1)S(1)}, u32[]{:S(2)}, u32[]{:S(2)}) async-start(bf16[64,6,128]{2,1,0:T(8,128)(2,1)} %copy.47), calls=%async_computation | async-start | bytes 262144 | tf_op jit(solution)/shard_map/all_to_all | solution.py:474
  36.9 0.1 iota_compare_fusion.3
  36.9 0.1 copy.43
  37.0 0.1 copy.45
  37.1 0.1 copy.46
  37.2 0.3 select_reduce_fusion
  37.5 0.1 reshape.81.surface_ref
  37.6 0.1 reshape.79.speeds_ref
  37.7 0.0 copy-done.5
  37.7 0.1 select_reduce_fusion.1
  37.8 0.1 reshape.83.wet_ref
  37.9 0.0 copy-done.4
  38.0 0.0 copy-done.3
  38.0 20.5 %wave_step.1 = bf16[384,1152]{1,0:T(8,128)(2,1)} custom-call(bf16[1152,512]{1,0:T(8,128)(2,1)S(1)} %get-tuple-element.7.win_ref, bf16[1152,128]{1,0:T(8,128)(2,1)S(1)} %get-tuple-element.8.edges_ref, f32[1,128]{1,0:T(1,128)S(1)} %select_convert_fusion.mask_ref, bf16[1152,128]{1,0:T(8,128)(2,1)S(1)} %get-tuple-element.9.kernel_ref, ...), custom_call_target="tpu_custom_call" | custom-call | flops 12230590464 | bytes 2359296 | tf_op jit(solution)/shard_map/wave_step/pallas_call | solution.py:371
  58.4 0.0 all-to-all-done.drift_ref
  58.4 1.0 %ocean_step.1 = f32[2,192,128]{2,1,0:T(8,128)} custom-call(f32[2,192,128]{2,1,0:T(8,128)S(1)} %copy-done, bf16[64,6,128]{2,1,0:T(8,128)(2,1)S(1)} %all-to-all-done.drift_ref, s32[2,192]{1,0:T(2,128)S(1)} %copy-done.2), custom_call_target="tpu_custom_call" | custom-call | tf_op jit(solution)/shard_map/ocean_step/pallas_call | solution.py:251
  (11 shorter events, 0.1 us)
Async XLA Ops:
  1.7 1.8 %copy-start.7 = (s32[32]{0:T(128)S(1)}, s32[32]{0:T(128)}, u32[]{:S(2)}) copy-start(s32[32]{0:T(128)} %param.15) | copy-start | bytes 388
  3.8 0.9 %copy-start = (f32[2,192,128]{2,1,0:T(8,128)S(1)}, f32[2,192,128]{2,1,0:T(8,128)}, u32[]{:S(2)}) copy-start(f32[2,192,128]{2,1,0:T(8,128)} %currents_ref.3) | copy-start | bytes 589828
  3.8 0.9 %copy-start.2 = (s32[2,192]{1,0:T(2,128)S(1)}, s32[2,192]{1,0:T(2,128)}, u32[]{:S(2)}) copy-start(s32[2,192]{1,0:T(2,128)} %wet_ref.3) | copy-start | bytes 4612
  3.8 1.5 %copy-start.6 = (f32[2,288]{1,0:T(2,128)S(1)}, f32[2,288]{1,0:T(2,128)}, u32[]{:S(2)}) copy-start(f32[2,288]{1,0:T(2,128)} %param.10) | copy-start | bytes 6916
  3.8 1.5 %copy-start.1 = (bf16[288,128]{1,0:T(8,128)(2,1)S(1)}, bf16[288,128]{1,0:T(8,128)(2,1)}, u32[]{:S(2)}) copy-start(bf16[288,128]{1,0:T(8,128)(2,1)} %table.1) | copy-start | bytes 221188
  31.7 6.0 %copy-start.5 = (s32[24,64]{1,0:T(8,128)S(1)}, s32[24,64]{1,0:T(8,128)}, u32[]{:S(2)}) copy-start(s32[24,64]{1,0:T(8,128)} %param.16) | copy-start | bytes 18436
  31.8 6.2 %copy-start.4 = (f32[4608]{0:T(1024)S(1)}, f32[4608]{0:T(1024)}, u32[]{:S(2)}) copy-start(f32[4608]{0:T(1024)} %param.13) | copy-start | bytes 55300
  31.8 6.2 %copy-start.3 = (s32[3,4608]{1,0:T(4,128)S(1)}, s32[3,4608]{1,0:T(4,128)}, u32[]{:S(2)}) copy-start(s32[3,4608]{1,0:T(4,128)} %ids_ref.1) | copy-start | bytes 165892
  33.2 25.2 %all-to-all-start = ((bf16[64,6,128]{2,1,0:T(8,128)(2,1)}), bf16[64,6,128]{2,1,0:T(8,128)(2,1)S(1)}, u32[]{:S(2)}, u32[]{:S(2)}) async-start(bf16[64,6,128]{2,1,0:T(8,128)(2,1)} %copy.47), calls=%async_computation | async-start | bytes 262144 | tf_op jit(solution)/shard_map/all_to_all | solution.py:474

commit v6 on v5

--- a/solution.py
+++ b/solution.py
@@ -93,9 +93,6 @@
         pltpu.make_async_copy(speeds, speeds_out.at[part], own_sem.at[2]),
         pltpu.make_async_copy(surface.at[me], surface_out.at[me], own_sem.at[3]),
     ]
-    for copy in own:
-        copy.start()
-
     barrier = pltpu.get_barrier_semaphore()
 
     def greet(k, carry):
@@ -111,7 +108,7 @@
     pl.semaphore_wait(barrier, total - 1)
 
     sends = []
-    for j in range(1, bins_count):
+    for j in sorted(range(1, bins_count), key=lambda j: abs(2 * j - bins_count)):
         peer = lax.rem(part + j, bins_count)
         device = (space, peer)
         sends.append(
@@ -129,7 +126,9 @@
                 device,
             )
         )
-    for copy in sends:
+    for copy in sends[2::3] + sends[1::3] + sends[0::3]:
+        copy.start()
+    for copy in own:
         copy.start()
 
     def up():

time: 59.9 us -> 59.7 us (level)
  transfers between devices with their start and end apart: 1 -> 1, of which waited for: 0 -> 0; matrix products, arithmetic and copies ran while one was open for 2% -> 2% of each run, Pallas kernels for 34% -> 35%
where the time goes in v6:
time: 59.7 us; the launch traced here: 59.2 us
  Pallas kernels  48.1 us (81%)
  local copies, waits for them, and re-layouts  5.02 us (8%)
  starting transfers between devices  3.81 us (6%)
  between operations  0.92 us (2%)
  other arithmetic  0.73 us (1%)
  matrix products  0.67 us (1%)
    pallas_call x1, Pallas kernels, exchange(): pl.pallas_call(functools.partial(exchange_kernel, space_count, bins_count...  26.1 us
    pallas_call x1, Pallas kernels, wave_step(): pl.pallas_call(functools.partial(wave_kernel, columns, chunk), grid=(pair...  20.5 us
    all_to_all x1, starting transfers between devices, per_device(): lax.all_to_all(routed, ('space', 'bins'), split_axis=0, concat_axis=0, ti...  3.81 us
    reshape x1, local copies, waits for them, and re-layouts, per_device(): rows = spectrum.reshape(local_bins, bins_count, width)  1.62 us
  transfers between devices with their start and end apart: 1, of which 0 were waited for; matrix products, arithmetic and copies ran while one was open for 2% of the time, Pallas kernels for 35%

profile of v6, /device:TPU:1, one launch (start us, length us, event | category | flops | bytes accessed | tf_op | source)
XLA Modules:
  0.0 59.2 jit_solution(13923671294603316751)
XLA Ops:
  0.6 0.8 %fusion.8 = (bf16[288,1,64]{0,2,1:T(8,128)(2,1)S(1)}, bf16[288,1,64]{0,2,1:T(8,128)(2,1)S(1)}) fusion(bf16[288,24,64]{0,2,1:T(8,128)(2,1)} %param.9), kind=kLoop, calls=%fused_computation.24 | loop fusion | bytes 147456 | tf_op jit(solution)/shard_map/slice | solution.py:435
  1.5 0.1 copy.48
  1.6 0.1 copy.49
  1.7 0.0 copy-start.7
  1.7 1.6 %copy.37 = bf16[288,4,384]{2,0,1:T(8,128)(2,1)S(1)} copy(bf16[288,4,384]{0,2,1:T(8,128)(2,1)} %bitcast.30) | data formatting | bytes 1769472 | tf_op jit(solution)/shard_map/reshape | solution.py:427
  3.4 0.1 fusion.9
  3.5 0.0 copy-done.7
  3.5 0.1 iota_add_fusion
  3.6 0.1 add.33
  3.7 0.1 pad_bitcast_fusion
  3.8 0.0 copy-start
  3.8 0.0 copy-start.2
  3.8 0.0 copy-start.6
  3.8 0.0 copy-start.1
  3.9 0.2 fusion.5.windows
  4.1 0.7 %copy-done = f32[2,192,128]{2,1,0:T(8,128)S(1)} copy-done((f32[2,192,128]{2,1,0:T(8,128)S(1)}, f32[2,192,128]{2,1,0:T(8,128)}, u32[]{:S(2)}) %copy-start) | copy-done | bytes 196632
  4.7 0.0 copy-done.2
  4.7 0.6 surface_windows.1
  5.3 0.0 copy-done.6
  5.4 0.0 copy-done.1
  5.4 26.1 %exchange.1 = (bf16[1152,512]{1,0:T(8,128)(2,1)S(1)}, bf16[1152,128]{1,0:T(8,128)(2,1)S(1)}, f32[4,8,384]{2,1,0:T(8,128)S(1)}, bf16[1152,128]{1,0:T(8,128)(2,1)S(1)}, f32[32,1,128]{2,1,0:T(1,128)S(1)}) custom-call(bf16[4,288,512]{2,1,0:T(8,128)(2,1)S(1)} %fusion.5.windows, bf16[288,128]{1,0:T(8,128)(2,1)S(1)} %copy-done.1, f32[8,384]{1,0:T(8,128)S(1)} %pad.8.speeds, ...), custom_call_target="tpu_custom_call" | custom-call | tf_op jit(solution)/shard_map/exchange/pallas_call | solution.py:202
  31.4 0.0 copy-start.5
  31.4 0.0 copy-start.4
  31.5 0.0 copy-start.3
  31.5 0.5 convolution_convert_fusion
  31.9 0.2 convolution_convert_fusion.1
  32.2 0.7 %copy.47 = bf16[64,6,128]{2,1,0:T(8,128)(2,1)} copy(bf16[64,6,128]{2,0,1:T(8,128)(2,1)S(1)} %convolution_convert_fusion.1) | data formatting | bytes 196608 | tf_op jit(solution)/shard_map/convert_element_type | solution.py:472
  32.9 3.8 %all-to-all-start = ((bf16[64,6,128]{2,1,0:T(8,128)(2,1)}), bf16[64,6,128]{2,1,0:T(8,128)(2,1)S(1)}, u32[]{:S(2)}, u32[]{:S(2)}) async-start(bf16[64,6,128]{2,1,0:T(8,128)(2,1)} %copy.47), calls=%async_computation | async-start | bytes 262144 | tf_op jit(solution)/shard_map/all_to_all | solution.py:473
  36.7 0.1 iota_compare_fusion.3
  36.8 0.1 copy.43
  36.9 0.1 copy.45
  37.0 0.1 copy.46
  37.1 0.3 select_reduce_fusion
  37.3 0.1 reshape.81.surface_ref
  37.4 0.1 reshape.79.speeds_ref
  37.5 0.0 copy-done.5
  37.6 0.1 select_reduce_fusion.1
  37.7 0.1 reshape.83.wet_ref
  37.7 0.0 copy-done.4
  37.8 0.0 copy-done.3
  37.8 20.5 %wave_step.1 = bf16[384,1152]{1,0:T(8,128)(2,1)} custom-call(bf16[1152,512]{1,0:T(8,128)(2,1)S(1)} %get-tuple-element.7.win_ref, bf16[1152,128]{1,0:T(8,128)(2,1)S(1)} %get-tuple-element.8.edges_ref, f32[1,128]{1,0:T(1,128)S(1)} %select_convert_fusion.mask_ref, bf16[1152,128]{1,0:T(8,128)(2,1)S(1)} %get-tuple-element.9.kernel_ref, ...), custom_call_target="tpu_custom_call" | custom-call | flops 12230590464 | bytes 2359296 | tf_op jit(solution)/shard_map/wave_step/pallas_call | solution.py:370
  58.3 0.0 all-to-all-done.drift_ref
  58.3 1.0 %ocean_step.1 = f32[2,192,128]{2,1,0:T(8,128)} custom-call(f32[2,192,128]{2,1,0:T(8,128)S(1)} %copy-done, bf16[64,6,128]{2,1,0:T(8,128)(2,1)S(1)} %all-to-all-done.drift_ref, s32[2,192]{1,0:T(2,128)S(1)} %copy-done.2), custom_call_target="tpu_custom_call" | custom-call | tf_op jit(solution)/shard_map/ocean_step/pallas_call | solution.py:250
  (11 shorter events, 0.1 us)
Async XLA Ops:
  1.7 1.8 %copy-start.7 = (s32[32]{0:T(128)S(1)}, s32[32]{0:T(128)}, u32[]{:S(2)}) copy-start(s32[32]{0:T(128)} %param.15) | copy-start | bytes 388
  3.8 0.9 %copy-start = (f32[2,192,128]{2,1,0:T(8,128)S(1)}, f32[2,192,128]{2,1,0:T(8,128)}, u32[]{:S(2)}) copy-start(f32[2,192,128]{2,1,0:T(8,128)} %currents_ref.3) | copy-start | bytes 589828
  3.8 0.9 %copy-start.2 = (s32[2,192]{1,0:T(2,128)S(1)}, s32[2,192]{1,0:T(2,128)}, u32[]{:S(2)}) copy-start(s32[2,192]{1,0:T(2,128)} %wet_ref.3) | copy-start | bytes 4612
  3.8 1.5 %copy-start.6 = (f32[2,288]{1,0:T(2,128)S(1)}, f32[2,288]{1,0:T(2,128)}, u32[]{:S(2)}) copy-start(f32[2,288]{1,0:T(2,128)} %param.10) | copy-start | bytes 6916
  3.8 1.5 %copy-start.1 = (bf16[288,128]{1,0:T(8,128)(2,1)S(1)}, bf16[288,128]{1,0:T(8,128)(2,1)}, u32[]{:S(2)}) copy-start(bf16[288,128]{1,0:T(8,128)(2,1)} %table.1) | copy-start | bytes 221188
  31.4 6.1 %copy-start.5 = (s32[24,64]{1,0:T(8,128)S(1)}, s32[24,64]{1,0:T(8,128)}, u32[]{:S(2)}) copy-start(s32[24,64]{1,0:T(8,128)} %param.16) | copy-start | bytes 18436
  31.4 6.3 %copy-start.4 = (f32[4608]{0:T(1024)S(1)}, f32[4608]{0:T(1024)}, u32[]{:S(2)}) copy-start(f32[4608]{0:T(1024)} %param.13) | copy-start | bytes 55300
  31.5 6.3 %copy-start.3 = (s32[3,4608]{1,0:T(4,128)S(1)}, s32[3,4608]{1,0:T(4,128)}, u32[]{:S(2)}) copy-start(s32[3,4608]{1,0:T(4,128)} %ids_ref.1) | copy-start | bytes 165892
  32.9 25.4 %all-to-all-start = ((bf16[64,6,128]{2,1,0:T(8,128)(2,1)}), bf16[64,6,128]{2,1,0:T(8,128)(2,1)S(1)}, u32[]{:S(2)}, u32[]{:S(2)}) async-start(bf16[64,6,128]{2,1,0:T(8,128)(2,1)} %copy.47), calls=%async_computation | async-start | bytes 262144 | tf_op jit(solution)/shard_map/all_to_all | solution.py:473
